TPU v7x, 32 devices: a whole 2x2x4 slice. The times are simulated.
32 devices in a mesh: dp: 4 (over y, core), seq: 4 (over z), chan: 2 (over x).
Axes of the slice: x: 2, y: 2, z: 4, core: 2. Of those that a mesh axis runs over, the one named last changes fastest.
Arguments:
- query_rows: bfloat16 [2048, 8192], P(('dp', 'seq'), 'chan'), may hold values from -6 to 6
- key_rows: bfloat16 [2048, 8192], P(('dp', 'seq'), 'chan'), may hold values from -6 to 6
- value_rows: bfloat16 [2048, 8192], P(('dp', 'seq'), 'chan'), may hold values from -6 to 6
- grad_rows: bfloat16 [2048, 8192], P(('dp', 'seq'), 'chan'), may hold values from -6 to 6
- filter_taps: float32 [512, 8192], P(None, ('chan', 'seq')), may hold values from -0.25 to 0.25
Outputs:
- grad_query: bfloat16 [2048, 8192], P(('dp', 'seq'), 'chan')
- grad_key: bfloat16 [2048, 8192], P(('dp', 'seq'), 'chan')
- grad_value: bfloat16 [2048, 8192], P(('dp', 'seq'), 'chan')
- grad_filter: float32 [512, 8192], P('dp', ('chan', 'seq'))
All inputs are finite; a program needn't handle non-finite values.
Results may differ from a plain program's by a relative error of at most 0.0059.
Values may be sent and summed in bfloat16 or wider, within the bound.
No kernel may reach another device: no remote copies, remote signals or barrier semaphores. Data moves between devices by JAX's collectives and lax.ppermute only.
A program may use at most 128 MiB of HBM per device.

v0:
```python
import functools

import jax
import jax.numpy as jnp
import ml_dtypes
import numpy as np
from jax import lax
from jax.experimental import pallas as pl
from jax.experimental.pallas import tpu as pltpu
from jax.sharding import PartitionSpec as P


def split_bf16(x):
    high = x.astype(ml_dtypes.bfloat16)
    return np.concatenate([high, (x - high.astype(np.float64)).astype(ml_dtypes.bfloat16)])


@functools.cache
def tables(half_len):
    freq = 2 * np.arange(half_len)[:, None] + 1
    angles = np.pi * (freq * np.arange(half_len)[None, :] % (4 * half_len)) / (2 * half_len)
    forward = np.concatenate([np.cos(angles), -np.sin(angles)], axis=0)
    both = [forward, forward[:, ::-1]]
    return (
        np.concatenate([split_bf16(m) for m in both]),
        np.concatenate([(m.T / half_len).astype(ml_dtypes.bfloat16) for m in both]),
    )


VMEM = 12 << 20
tiny = pl.CostEstimate(flops=0, bytes_accessed=1, transcendentals=0)
large = pl.CostEstimate(flops=1 << 35, bytes_accessed=1, transcendentals=0)


def hop(half, across, steps):
    return [
        (h * half + p, (h ^ across) * half + (p + steps) % half)
        for h in (0, 1)
        for p in range(half)
    ]


def flip(size, bit):
    return [(d, d ^ bit) for d in range(size)]


def after(place, steps, half):
    return lax.rem(place + steps, half)


def before(place, steps, half):
    return lax.rem(place + half - steps, half)


def group_of(info, place, other, half):
    side = 1 - info[0] if other else info[0]
    return side * half + place


def gate_kernel(half, spans, info, *refs):
    inputs, taps, outputs = refs[: 8 * half], refs[8 * half], refs[8 * half + 1 :]
    lower = info[0] == 0
    outputs[-1][...] = taps[...].astype(jnp.bfloat16)
    for r in range(half):
        for t in (0, 1):
            query, key, value, grad = (
                ref[...].astype(jnp.float32) for ref in inputs[8 * r + 4 * t : 8 * r + 4 * t + 4]
            )
            mixed, scaled = key * value, grad * query
            first = jnp.where(lower, mixed, scaled).astype(jnp.bfloat16)
            second = jnp.where(lower, scaled, mixed).astype(jnp.bfloat16)
            for chunk, cols in enumerate(spans):
                outputs[chunk * 2 * half + r][t] = first[:, cols]
                outputs[chunk * 2 * half + r][2 + t] = second[:, cols]
                if t:
                    outputs[chunk * 2 * half + half + r][...] = first[:, cols]


def gate(info, half, spans, rows, taps):
    tokens, channels = rows[0].shape
    group = channels // (2 * half)
    piece = taps.shape[0] // 4

    def column(i, info, r, t):
        return (0, group_of(info, after(info[1], r, half), t, half))

    in_specs = [
        pl.BlockSpec((tokens, group), functools.partial(column, r=r, t=t))
        for r in range(half)
        for t in (0, 1)
        for _ in range(4)
    ]
    in_specs.append(pl.BlockSpec((piece, group), lambda i, info: (info[2] % 2, 0)))
    shapes = []
    for cols in spans:
        width = cols.stop - cols.start
        shapes += [(4, tokens, width)] * half + [(tokens, width)] * half
    shapes.append((piece, group))
    outs = pl.pallas_call(
        functools.partial(gate_kernel, half, spans),
        grid_spec=pltpu.PrefetchScalarGridSpec(
            num_scalar_prefetch=1,
            grid=(1,),
            in_specs=in_specs,
            out_specs=[
                pl.BlockSpec(s, lambda i, info, n=len(s): (0,) * n) for s in shapes
            ],
        ),
        out_shape=[jax.ShapeDtypeStruct(s, jnp.bfloat16) for s in shapes],
        compiler_params=pltpu.CompilerParams(vmem_limit_bytes=56 << 20),
        cost_estimate=tiny,
    )(info, *(list(rows) * (2 * half)), taps)
    parts = [outs[2 * half * c : 2 * half * (c + 1)] for c in range(len(spans))]
    return [x[:half] for x in parts], [x[half:] for x in parts], outs[-1]


def high_low(x):
    high = x.astype(jnp.bfloat16)
    return high, (x - high.astype(jnp.float32)).astype(jnp.bfloat16)


def dot(a, b):
    return jnp.dot(a, b, preferred_element_type=jnp.float32)


def times(a, b):
    return a[0] * b[0] - a[1] * b[1], a[0] * b[1] + a[1] * b[0]


def conj_times(a, b):
    return a[0] * b[0] + a[1] * b[1], a[0] * b[1] - a[1] * b[0]


def plus(a, b):
    return a[0] + b[0], a[1] + b[1]


def load(ref, j, re, im, width):
    cols = slice(j * width, (j + 1) * width)
    return ref[re, cols], ref[im, cols]


def store(ref, j, re, im, x):
    width = x[0].shape[1]
    cols = slice(j * width, (j + 1) * width)
    ref[re, cols] = x[0].astype(ref.dtype)
    ref[im, cols] = x[1].astype(ref.dtype)


def by_strips(length, width, body):
    strip = 16
    odd = lax.broadcasted_iota(jnp.int32, (strip, width), 0) % 2
    sign = (1 - 2 * odd).astype(jnp.float32)

    def late(x):
        return sign * x[1], -sign * x[0]

    def early(x):
        return -sign * x[1], sign * x[0]

    def step(i, carry):
        re = pl.ds(pl.multiple_of(i * strip, strip), strip)
        im = pl.ds(pl.multiple_of(length + i * strip, strip), strip)
        body(re, im, late, early)
        return carry

    lax.fori_loop(0, length // strip, step, 0, unroll=4)


def chosen(table, side):
    rows = table.shape[0] // 2
    return table[pl.ds(pl.multiple_of(side * rows, rows), rows), :]


def transform(matrix, x):
    rows = matrix.shape[0] // 2
    return dot(matrix[:rows], x) + dot(matrix[rows:], x)


def place_rows(target, j, sources, cols, place, half):
    block, width = sources[0].shape[0], cols.stop - cols.start
    for r, source in enumerate(sources):
        rows = pl.ds(pl.multiple_of(before(place, r, half) * block, block), block)
        target[rows, j * width : (j + 1) * width] = source[:, cols]


def split_lags(grads, j, keep, cols, send, row, replicas, core):
    lags, width = 2 * grads.shape[0] // replicas, cols.stop - cols.start
    for ref, cols, mine in ((keep, cols, core), (send, slice(0, width), 1 - core)):
        for i in range(replicas // 4):
            rows = pl.ds(pl.multiple_of((2 * i + mine) * lags, lags), lags)
            part = grads[rows, j * width : (j + 1) * width]
            ref[row + i * lags : row + (i + 1) * lags, cols] = part.astype(ref.dtype)


def taps_kernel(tile, info, taps, fwd, near_spec, all_spec, high, low):
    length = taps.shape[0] // 2
    matrix = chosen(fwd, 0)
    for cols in tiles(taps.shape[1], tile):
        for j in (0, 1):
            part = slice(j * tile, (j + 1) * tile)
            high[:, part], low[:, part] = high_low(taps[j * length : (j + 1) * length, cols])
        spec = transform(matrix, high[...]) + dot(matrix[: 2 * length], low[...])
        near_spec[:, cols] = spec[:, :tile]
        all_spec[:, cols] = spec[:, tile:]

        def body(re, im, late, early, cols=cols):
            far = late((all_spec[re, cols], all_spec[im, cols]))
            all_spec[re, cols] = near_spec[re, cols] + far[0]
            all_spec[im, cols] = near_spec[im, cols] + far[1]

        by_strips(length, tile, body)


def conv_kernel(half, replicas, start, tile, info, *refs):
    pairs, crosses, refs = refs[:half], refs[half : 2 * half], refs[2 * half :]
    tap_spec, tap_all, *near, fwd, inv = refs[:6]
    refs = refs[7 if start else 6 :]
    pair_outs, cross_outs, keep = refs[:half], refs[half : 2 * half], refs[2 * half]
    *sends, data, near_all, spec, near_spec, high, conv, grads = refs[2 * half + 1 :]
    side, place, core = info[0], info[1], info[2] % 2
    _, block, width = pairs[0].shape
    length = half * block
    piece = length // 2
    fwd_data, inv_data = chosen(fwd, side), chosen(inv, side)
    for cols, send in zip(tiles(width, tile), sends, strict=True):
        wide = cols.stop - cols.start
        whole = slice(start + cols.start, start + cols.stop)
        for j in range(4):
            place_rows(data, j, [pair.at[j] for pair in pairs], cols, place, half)
        place_rows(data, 4, crosses, cols, place, half)
        for j in (0, 1):
            rows = pl.ds(pl.multiple_of((core ^ j) * piece, piece), piece)
            near_all[rows, :wide] = near[j][:, whole]
        spec[:, : 5 * wide] = transform(fwd_data, data[:, : 5 * wide])
        near_spec[:, :wide] = transform(chosen(fwd, 0), near_all[:, :wide])

        def body(re, im, late, early, whole=whole, wide=wide):
            a_own, a_other, c_own, c_other = (load(spec, j, re, im, wide) for j in range(4))
            c_far = late(load(spec, 4, re, im, wide))
            h_own, h_all = ((x[re, whole], x[im, whole]) for x in (tap_spec, tap_all))
            h_other = load(near_spec, 0, re, im, wide)
            store(high, 0, re, im, times(a_own, h_own))
            store(high, 1, re, im, times(a_other, h_other))
            store(high, 2, re, im, plus(conj_times(h_own, c_own), conj_times(h_all, c_far)))
            store(high, 3, re, im, conj_times(h_other, c_other))
            store(high, 4, re, im, early(times(a_own, h_all)))
            store(high, 5, re, im, conj_times(a_own, plus(c_own, c_far)))
            store(high, 6, re, im, early(conj_times(a_own, c_far)))
            store(high, 7, re, im, conj_times(a_other, c_other))

        by_strips(length, wide, body)
        conv[:, : 5 * wide] = dot(inv_data, high[:, : 5 * wide]).astype(jnp.bfloat16)
        grads[:, : 3 * wide] = dot(chosen(inv, 0), high[:, 5 * wide : 8 * wide])
        for r in range(half):
            rows = pl.ds(pl.multiple_of(after(place, r, half) * block, block), block)
            for j in range(4):
                pair_outs[r][j, :, cols] = conv[rows, j * wide : (j + 1) * wide]
            cross_outs[r][:, cols] = conv[rows, 4 * wide : 5 * wide]
        for j in range(3):
            split_lags(grads, j, keep, whole, send, j * length // 2, replicas, core)


def tiles(width, tile):
    return [slice(i, min(i + tile, width)) for i in range(0, width, tile)]


def spectral(kernel, tile, info, operands, shapes, scratch, cost, aliases={}):
    tile = min(tile, shapes[0][0][-1])
    vmem = pl.BlockSpec(memory_space=pltpu.VMEM)
    return pl.pallas_call(
        functools.partial(kernel, tile),
        in_specs=[pl.BlockSpec(memory_space=pltpu.SMEM)] + [vmem] * len(operands),
        out_specs=[vmem] * len(shapes),
        scratch_shapes=[pltpu.VMEM((r, n * tile), t) for r, n, t in scratch],
        out_shape=[jax.ShapeDtypeStruct(s, t) for s, t in shapes],
        compiler_params=pltpu.CompilerParams(vmem_limit_bytes=VMEM),
        input_output_aliases=aliases,
        cost_estimate=cost,
    )(info, *operands)


def finish_kernel(half, start, info, *refs):
    received = refs[: 2 * half]
    grad, value, key = refs[2 * half : 2 * half + 3]
    *outs, made, sems = refs[-5:]
    lower = info[0] == 0
    width = made.shape[3]
    group = grad.shape[1] // (2 * half)
    copies = []
    for s in range(2 * half):
        r, other = s // 2, s % 2
        pair, cross = received[r], received[half + r]
        col = group_of(info, before(info[1], r, half), other, half) * group + start
        cols = pl.ds(pl.multiple_of(col, 128), width)
        first = pair[other].astype(jnp.float32)
        second = pair[2 + other].astype(jnp.float32)
        if other:
            second += cross[...].astype(jnp.float32)
            second = second.astype(jnp.bfloat16).astype(jnp.float32)
        conv = jnp.where(lower, first, second)
        back = jnp.where(lower, second, first)
        for i, (x, row) in enumerate(((conv, grad), (back, value), (back, key))):
            made[i, s] = (x * row[:, cols].astype(jnp.float32)).astype(jnp.bfloat16)
            copies.append(pltpu.make_async_copy(made.at[i, s], outs[i].at[:, cols], sems.at[i, s]))
            copies[-1].start()
    for copy in copies:
        copy.wait()


def finish(info, half, start, pairs, crosses, grad, value, key, earlier):
    tokens, width = crosses[0].shape
    vmem, anywhere = pl.BlockSpec(memory_space=pltpu.VMEM), pl.BlockSpec(memory_space=pl.ANY)
    return pl.pallas_call(
        functools.partial(finish_kernel, half, start),
        in_specs=[pl.BlockSpec(memory_space=pltpu.SMEM)]
        + [vmem] * (2 * half + 3)
        + [anywhere] * len(earlier),
        out_specs=[anywhere] * 3,
        out_shape=[jax.ShapeDtypeStruct(grad.shape, jnp.bfloat16)] * 3,
        scratch_shapes=[
            pltpu.VMEM((3, 2 * half, tokens, width), jnp.bfloat16),
            pltpu.SemaphoreType.DMA((3, 2 * half)),
        ],
        input_output_aliases={2 * half + 4 + i: i for i in range(len(earlier))},
        compiler_params=pltpu.CompilerParams(vmem_limit_bytes=VMEM),
        cost_estimate=large if earlier else tiny,
    )(info, *pairs, *crosses, grad, value, key, *earlier)


def sum_kernel(keep, *refs):
    *sends, own, other = refs
    rows = own.shape[0]
    start = 0
    for send in sends:
        cols = slice(start, start + send.shape[1])
        start = cols.stop
        own[:, cols] = keep[:rows, cols] + send[:rows, :].astype(jnp.float32)
        total = keep[rows:, cols] + send[rows:, :].astype(jnp.float32)
        other[:, cols] = total.astype(other.dtype)


def last_kernel(bit, info, own, over, go, stay):
    upper = info[2] & bit != 0
    first, second = own[0] + over[...].astype(jnp.float32), own[1]
    go[...] = jnp.where(upper, first, second).astype(go.dtype)
    stay[...] = jnp.where(upper, second, first)


def halve(x, bit, replicas, wire):
    upper = lax.axis_index("dp") & bit != 0
    x = x.reshape(-1, 2, *x.shape[1:])
    go = jnp.where(upper, x[:, 0], x[:, 1]).astype(wire)
    stay = jnp.where(upper, x[:, 1], x[:, 0])
    return stay + lax.ppermute(go, "dp", flip(replicas, bit)).astype(jnp.float32)


def sum_lags(keep, sends, length, replicas):
    sends = [lax.ppermute(x, "dp", flip(replicas, 1)) for x in sends]
    vmem = pl.BlockSpec(memory_space=pltpu.VMEM)
    width = keep.shape[1]
    own, other = pl.pallas_call(
        sum_kernel,
        in_specs=[vmem] * (1 + len(sends)),
        out_specs=[vmem, vmem],
        out_shape=[
            jax.ShapeDtypeStruct((length, width), jnp.float32),
            jax.ShapeDtypeStruct(
                (length // 2, width), jnp.bfloat16 if replicas == 4 else jnp.float32
            ),
        ],
        compiler_params=pltpu.CompilerParams(vmem_limit_bytes=VMEM),
        cost_estimate=tiny,
    )(keep, *sends)
    lags = 2 * length // replicas
    own, other = own.reshape(-1, lags, width), other.reshape(-1, lags, width)
    bit = 2
    while bit < replicas // 2:
        own, other = (halve(x, bit, replicas, jnp.float32) for x in (own, other))
        bit *= 2
    return own, other[0].astype(jnp.bfloat16)


def local(replicas, half, query, key, value, grad, taps):
    place = lax.axis_index("seq")
    info = jnp.stack([place // half, place % half, lax.axis_index("dp")]).astype(jnp.int32)
    length, width = taps.shape[0] // 2, taps.shape[1]
    block = query.shape[0]
    f32, bf16 = jnp.float32, jnp.bfloat16
    forward, inverse = (jnp.asarray(t) for t in tables(length))

    def pass_on(pairs):
        return [lax.ppermute(x, "seq", hop(half, 0, r)) if r else x for r, x in enumerate(pairs)]

    def pass_over(crosses):
        return [lax.ppermute(x, "seq", hop(half, 1, r)) for r, x in enumerate(crosses)]

    cut = width * 5 // 8 // 128 * 128
    spans = [slice(0, cut), slice(cut, width)] if cut else [slice(0, width)]
    pairs, crosses, near = gate(info, half, spans, (query, key, value, grad), taps)
    near = lax.ppermute(near, "seq", hop(half, 1, 0))
    tap_specs = spectral(
        taps_kernel,
        256,
        info,
        [taps, forward],
        [((2 * length, width), f32)] * 2,
        [(length, 2, bf16), (length, 2, bf16)],
        tiny,
    )
    pairs, crosses[0] = [pass_on(x) for x in pairs], pass_over(crosses[0])
    for c in range(1, len(spans)):
        crosses[c], (pairs[0], crosses[0], near, tap_specs) = lax.optimization_barrier(
            (crosses[c], (pairs[0], crosses[0], near, tap_specs))
        )
        crosses[c] = pass_over(crosses[c])
    near = (near, lax.ppermute(near, "dp", flip(replicas, 1)))
    results, cross_results, keep, sends = [], [], [], []
    for c, cols in enumerate(spans):
        wide = cols.stop - cols.start
        outs = spectral(
            functools.partial(conv_kernel, half, replicas, cols.start),
            256,
            info,
            [*pairs[c], *crosses[c], *tap_specs, *near, forward, inverse, *keep],
            [((4, block, wide), bf16)] * half
            + [((block, wide), bf16)] * half
            + [((3 * length // 2, width), f32)]
            + [((3 * length // 2, t.stop - t.start), bf16) for t in tiles(wide, 256)],
            [
                (length, 5, bf16),
                (length, 1, bf16),
                (2 * length, 5, f32),
                (2 * length, 1, f32),
                (2 * length, 8, bf16),
                (length, 5, bf16),
                (length, 3, f32),
            ],
            large,
            {2 * half + 7: 2 * half} if c else {},
        )
        keep, *more = outs[2 * half :]
        keep, sends = [keep], sends + more
        cross = list(outs[half : 2 * half])
        if c:
            sends, cross_results[-1] = lax.optimization_barrier((sends, cross_results[-1]))
            cross[-1], results[-1] = lax.optimization_barrier((cross[-1], results[-1]))
        results.append(pass_on(outs[:half]))
        cross_results.append(pass_over(cross))
    own, other = sum_lags(*keep, sends, length, replicas)
    other = lax.ppermute(other, "seq", hop(half, 1, 0))
    outs = []
    for c, cols in enumerate(spans):
        outs = finish(info, half, cols.start, results[c], cross_results[c], grad, value, key, outs)
    vmem = pl.BlockSpec(memory_space=pltpu.VMEM)
    bit = replicas // 2
    go, stay = pl.pallas_call(
        functools.partial(last_kernel, bit),
        in_specs=[pl.BlockSpec(memory_space=pltpu.SMEM), vmem, vmem],
        out_specs=[vmem, vmem],
        out_shape=[jax.ShapeDtypeStruct(other.shape, t) for t in (bf16, f32)],
        compiler_params=pltpu.CompilerParams(vmem_limit_bytes=VMEM),
        cost_estimate=tiny,
    )(info, own, other)
    grad_filter = stay + lax.ppermute(go, "dp", flip(replicas, bit)).astype(f32)
    return *outs, grad_filter


def solution(mesh):
    rows = P(("dp", "seq"), "chan")
    return jax.shard_map(
        functools.partial(local, mesh.shape["dp"], mesh.shape["seq"] // 2),
        mesh=mesh,
        in_specs=(rows, rows, rows, rows, P(None, ("chan", "seq"))),
        out_specs=(rows, rows, rows, P("dp", ("chan", "seq"))),
        check_vma=False,
    )
```

profile of v0, /device:TPU:0, one launch (start us, length us, event | category | flops | bytes accessed | tf_op | source)
XLA Modules:
  0.0 97.7 jit_solution(16346380568267017810)
XLA Ops:
  0.6 0.7 pad_add_fusion.info
  1.3 5.1 %shard_map.102 = (bf16[4,128,640]{2,1,0:T(8,128)(2,1)}, bf16[4,128,640]{2,1,0:T(8,128)(2,1)}, bf16[128,640]{1,0:T(8,128)(2,1)}, bf16[128,640]{1,0:T(8,128)(2,1)}...) custom-call(s32[3]{0:T(128)} %pad_add_fusion.info, ...), custom_call_target="tpu_custom_call" | custom-call | bytes 1 | tf_op jit(solution)/shard_map/pallas_call | solution.py:99
  6.4 0.0 copy-start.9
  6.4 0.0 copy-start.6
  6.4 0.0 copy-start.8
  6.4 3.1 %collective-permute-start.1 = (bf16[4,128,640]{2,1,0:T(8,128)(2,1)}, bf16[4,128,640]{2,1,0:T(8,128)(2,1)S(1)}, u32[]{:S(2)}, u32[]{:S(2)}) collective-permute-start(bf16[4,128,640]{2,1,0:T(8,128)(2,1)} %get-tuple-element.64), channel_id=1, source_target_pairs={{0,2},{2,0},{4,6},{6,4},{1,3},{3,1},{5,7},{7,5},{8,10},{10,8},{12,... | collective-permute-start | bytes 1966088 | tf_op jit(solution)/shard_map/ppermute | solution.py:393
  9.5 2.6 %collective-permute-start.4 = (bf16[128,1024]{1,0:T(8,128)(2,1)}, bf16[128,1024]{1,0:T(8,128)(2,1)S(1)}, u32[]{:S(2)}, u32[]{:S(2)}) collective-permute-start(bf16[128,1024]{1,0:T(8,128)(2,1)} %get-tuple-element.67), channel_id=1, source_target_pairs={{0,4},{2,6},{4,0},{6,2},{1,5},{3,7},{5,1},{7,3},{8,12},{10,14},{12... | collective-permute-start | bytes 786440 | tf_op jit(solution)/shard_map/ppermute | solution.py:401
  12.1 0.3 collective-permute-start.2
  12.5 2.5 %collective-permute-start.3 = (bf16[128,640]{1,0:T(8,128)(2,1)}, bf16[128,640]{1,0:T(8,128)(2,1)S(1)}, u32[]{:S(2)}, u32[]{:S(2)}) collective-permute-start(bf16[128,640]{1,0:T(8,128)(2,1)} %get-tuple-element.66), channel_id=1, source_target_pairs={{0,6},{2,4},{4,2},{6,0},{1,7},{3,5},{5,3},{7,1},{8,14},{10,12},{12... | collective-permute-start | bytes 491528 | tf_op jit(solution)/shard_map/ppermute | solution.py:396
  14.9 3.4 %shard_map.103 = (f32[512,1024]{1,0:T(8,128)S(1)}, f32[512,1024]{1,0:T(8,128)S(1)}) custom-call(s32[3]{0:T(128)S(1)} %copy-done.5, f32[512,1024]{1,0:T(8,128)S(1)} %copy-done.3, bf16[2048,256]{1,0:T(8,128)(2,1)S(1)} %copy-done.4), custom_call_target="tpu_custom_call" | custom-call | bytes 1 | tf_op jit(solution)/shard_map/pallas_call | solution.py:271
  18.3 15.8 %collective-permute-done.2.refs_2_ = bf16[128,640]{1,0:T(8,128)(2,1)S(1)} collective-permute-done((bf16[128,640]{1,0:T(8,128)(2,1)}, bf16[128,640]{1,0:T(8,128)(2,1)S(1)}, u32[]{:S(2)}, u32[]{:S(2)}) %collective-permute-start.2) | collective-permute-done | bytes 163872 | tf_op jit(solution)/shard_map/ppermute | solution.py:396
  34.1 5.2 %collective-permute-done.3.refs_3_ = bf16[128,640]{1,0:T(8,128)(2,1)S(1)} collective-permute-done((bf16[128,640]{1,0:T(8,128)(2,1)}, bf16[128,640]{1,0:T(8,128)(2,1)S(1)}, u32[]{:S(2)}, u32[]{:S(2)}) %collective-permute-start.3) | collective-permute-done | bytes 163872 | tf_op jit(solution)/shard_map/ppermute | solution.py:396
  39.3 0.0 collective-permute-done.4.refs_6_
  39.3 0.0 collective-permute-done.1.refs_1_
  39.3 0.0 collective-permute-start.7
  39.3 0.0 copy-start.7
  39.3 0.1 collective-permute-start
  39.4 2.1 %collective-permute-start.5 = (bf16[128,384]{1,0:T(8,128)(2,1)S(1)}, bf16[128,384]{1,0:T(8,128)(2,1)S(1)}, u32[]{:S(2)}, u32[]{:S(2)}) collective-permute-start(bf16[128,384]{1,0:T(8,128)(2,1)S(1)} %copy-done.11), channel_id=1, source_target_pairs={{0,4},{2,6},{4,0},{6,2},{1,5},{3,7},{5,1},{7,3},{8,12},{10,14},{12... | collective-permute-start | bytes 294920 | tf_op jit(solution)/shard_map/ppermute | solution.py:396
  41.5 2.3 %collective-permute-start.6 = (bf16[128,384]{1,0:T(8,128)(2,1)S(1)}, bf16[128,384]{1,0:T(8,128)(2,1)S(1)}, u32[]{:S(2)}, u32[]{:S(2)}) collective-permute-start(bf16[128,384]{1,0:T(8,128)(2,1)S(1)} %copy-done.10), channel_id=1, source_target_pairs={{0,6},{2,4},{4,2},{6,0},{1,7},{3,5},{5,3},{7,1},{8,14},{10,12},{12... | collective-permute-start | bytes 294920 | tf_op jit(solution)/shard_map/ppermute | solution.py:396
  43.8 7.5 %shard_map.104 = (bf16[4,128,640]{2,1,0:T(8,128)(2,1)S(1)}, bf16[4,128,640]{2,1,0:T(8,128)(2,1)S(1)}, bf16[128,640]{1,0:T(8,128)(2,1)S(1)}, bf16[128,640]{1,0:T(...) custom-call(s32[3]{0:T(128)S(1)} %copy-done.5, ...), custom_call_target="tpu_custom_call" | custom-call | flops 34359738368 | bytes 1 | tf_op jit(solution)/shard_map/pallas_call | solution.py:271
  51.3 0.1 collective-permute-start.12
  51.4 1.7 %collective-permute-start.13 = (bf16[128,640]{1,0:T(8,128)(2,1)S(1)}, bf16[128,640]{1,0:T(8,128)(2,1)S(1)}, u32[]{:S(2)}, u32[]{:S(2)}) collective-permute-start(bf16[128,640]{1,0:T(8,128)(2,1)S(1)} %get-tuple-element.95), channel_id=1, source_target_pairs={{0,6},{2,4},{4,2},{6,0},{1,7},{3,5},{5,3},{7,1},{8,14},{10,12},{12... | collective-permute-start | bytes 491528 | tf_op jit(solution)/shard_map/ppermute | solution.py:396
  53.1 1.9 %collective-permute-done.refs_1_ = bf16[4,128,384]{2,1,0:T(8,128)(2,1)S(1)} collective-permute-done((bf16[4,128,384]{2,1,0:T(8,128)(2,1)S(1)}, bf16[4,128,384]{2,1,0:T(8,128)(2,1)S(1)}, u32[]{:S(2)}, u32[]{:S(2)}) %collective-permute-start) | collective-permute-done | bytes 393248 | tf_op jit(solution)/shard_map/ppermute | solution.py:393
  55.0 0.2 collective-permute-done.6.refs_3_
  55.3 5.0 %shard_map.105 = (bf16[4,128,384]{2,1,0:T(8,128)(2,1)S(1)}, bf16[4,128,384]{2,1,0:T(8,128)(2,1)S(1)}, bf16[128,384]{1,0:T(8,128)(2,1)S(1)}, bf16[128,384]{1,0:T(...) custom-call(s32[3]{0:T(128)S(1)} %copy-done.5, ...), custom_call_target="tpu_custom_call", output_to_operand_aliasing={{4}: (11, {})} | custom-call | flops 34359738368 | bytes 1 | tf_op jit(solution)/shard_map/pallas_call | solution.py:271
  60.2 0.0 copy-start
  60.2 0.0 copy-start.1
  60.2 0.0 copy-start.2
  60.3 5.3 %collective-permute-done.12.refs_2_ = bf16[128,640]{1,0:T(8,128)(2,1)S(1)} collective-permute-done((bf16[128,640]{1,0:T(8,128)(2,1)S(1)}, bf16[128,640]{1,0:T(8,128)(2,1)S(1)}, u32[]{:S(2)}, u32[]{:S(2)}) %collective-permute-start.12) | collective-permute-done | bytes 163872 | tf_op jit(solution)/shard_map/ppermute | solution.py:396
  65.6 0.5 collective-permute-start.18
  66.1 0.0 collective-permute-start.14
  66.1 0.5 collective-permute-start.15
  66.6 0.3 collective-permute-done.16.refs_2_
  66.9 0.2 collective-permute-start.17
  67.1 4.0 %collective-permute-start.8 = (bf16[4,128,384]{2,1,0:T(8,128)(2,1)S(1)}, bf16[4,128,384]{2,1,0:T(8,128)(2,1)S(1)}, u32[]{:S(2)}, u32[]{:S(2)}) collective-permute-start(bf16[4,128,384]{2,1,0:T(8,128)(2,1)S(1)} %get-tuple-element.81), channel_id=1, source_target_pairs={{0,2},{2,0},{4,6},{6,4},{1,3},{3,1},{5,7},{7,5},{8,10},{10,8},{12,... | collective-permute-start | bytes 1179656 | tf_op jit(solution)/shard_map/ppermute | solution.py:393
  71.1 0.2 shard_map.108
  71.3 2.1 %collective-permute-start.19 = (bf16[128,1024]{1,0:T(8,128)(2,1)S(1)}, bf16[128,1024]{1,0:T(8,128)(2,1)S(1)}, u32[]{:S(2)}, u32[]{:S(2)}) collective-permute-start(bf16[128,1024]{1,0:T(8,128)(2,1)S(1)} %get-tuple-element.111), channel_id=1, source_target_pairs={{0,4},{2,6},{4,0},{6,2},{1,5},{3,7},{5,1},{7,3},{8,12},{10,14},{12... | collective-permute-start | bytes 786440 | tf_op jit(solution)/shard_map/ppermute | solution.py:451
  73.4 0.9 collective-permute-start.9
  74.3 12.9 %collective-permute-done.10.refs_1_ = bf16[4,128,640]{2,1,0:T(8,128)(2,1)S(1)} collective-permute-done((bf16[4,128,640]{2,1,0:T(8,128)(2,1)S(1)}, bf16[4,128,640]{2,1,0:T(8,128)(2,1)S(1)}, u32[]{:S(2)}, u32[]{:S(2)}) %collective-permute-start.10) | collective-permute-done | bytes 655392 | tf_op jit(solution)/shard_map/ppermute | solution.py:393
  87.2 0.5 collective-permute-start.11
  87.6 0.7 collective-permute-done.19.over
  88.4 0.7 shard_map.109
  89.0 1.6 %collective-permute-start.20 = (bf16[128,1024]{1,0:T(8,128)(2,1)S(1)}, bf16[128,1024]{1,0:T(8,128)(2,1)S(1)}, u32[]{:S(2)}, u32[]{:S(2)}) collective-permute-start(bf16[128,1024]{1,0:T(8,128)(2,1)S(1)} %get-tuple-element.113), channel_id=1, source_target_pairs={{0,16},{8,24},{16,0},{24,8},{1,17},{9,25},{17,1},{25,9},{2,18},{10... | collective-permute-start | bytes 786440 | tf_op jit(solution)/shard_map/ppermute | solution.py:465
  90.6 2.1 %shard_map.106 = (bf16[128,4096]{1,0:T(8,128)(2,1)}, bf16[128,4096]{1,0:T(8,128)(2,1)}, bf16[128,4096]{1,0:T(8,128)(2,1)}) custom-call(s32[3]{0:T(128)S(1)} %copy-done.5, bf16[4,128,640]{2,1,0:T(8,128)(2,1)S(1)} %get-tuple-element.87.refs_0_, bf16[4,128,640]{2,1,0:T(8,128)(2,1)S(1)} %collective-permute-done.10.refs_1_, ...), custom_call_target="tpu_custom_call" | custom-call | bytes 1 | tf_op jit(solution)/shard_map/pallas_call | solution.py:314
  92.7 1.8 %collective-permute-done.11.refs_3_ = bf16[128,384]{1,0:T(8,128)(2,1)S(1)} collective-permute-done((bf16[128,384]{1,0:T(8,128)(2,1)S(1)}, bf16[128,384]{1,0:T(8,128)(2,1)S(1)}, u32[]{:S(2)}, u32[]{:S(2)}) %collective-permute-start.11) | collective-permute-done | bytes 98336 | tf_op jit(solution)/shard_map/ppermute | solution.py:396
  94.5 1.7 %shard_map.107 = (bf16[128,4096]{1,0:T(8,128)(2,1)}, bf16[128,4096]{1,0:T(8,128)(2,1)}, bf16[128,4096]{1,0:T(8,128)(2,1)}) custom-call(s32[3]{0:T(128)S(1)} %copy-done.5, bf16[4,128,384]{2,1,0:T(8,128)(2,1)S(1)} %get-tuple-element.80.refs_0_, ...), custom_call_target="tpu_custom_call", output_to_operand_aliasing={{0}: (8, {}), {1}: (9, {}), {2}: (10, {})} | custom-call | flops 34359738368 | bytes 1 | tf_op jit(solution)/shard_map/pallas_call | solution.py:314
  96.2 0.6 collective-permute-done.20
  96.8 0.8 convert_add_fusion
  (28 shorter events, 0.1 us)
Async XLA Ops:
  1.3 13.6 %copy-start.3 = (f32[512,1024]{1,0:T(8,128)S(1)}, f32[512,1024]{1,0:T(8,128)}, u32[]{:S(2)}) copy-start(f32[512,1024]{1,0:T(8,128)} %taps.1) | copy-start | bytes 6291460
  1.3 13.6 %copy-start.4 = (bf16[2048,256]{1,0:T(8,128)(2,1)S(1)}, bf16[2048,256]{1,0:T(8,128)(2,1)}, u32[]{:S(2)}) copy-start(bf16[2048,256]{1,0:T(8,128)(2,1)} %constant.37.clone.fwd.refs_8_) | copy-start | bytes 3145732
  1.3 13.6 %copy-start.5 = (s32[3]{0:T(128)S(1)}, s32[3]{0:T(128)}, u32[]{:S(2)}) copy-start(s32[3]{0:T(128)} %pad_add_fusion.info) | copy-start | bytes 40
  6.4 32.9 %copy-start.9 = (bf16[4,128,384]{2,1,0:T(8,128)(2,1)S(1)}, bf16[4,128,384]{2,1,0:T(8,128)(2,1)}, u32[]{:S(2)}) copy-start(bf16[4,128,384]{2,1,0:T(8,128)(2,1)} %get-tuple-element.60) | copy-start | bytes 1179652
  6.4 33.0 %copy-start.11 = (bf16[128,384]{1,0:T(8,128)(2,1)S(1)}, bf16[128,384]{1,0:T(8,128)(2,1)}, u32[]{:S(2)}) copy-start(bf16[128,384]{1,0:T(8,128)(2,1)} %get-tuple-element.70) | copy-start | bytes 294916
  6.4 35.1 %copy-start.10 = (bf16[128,384]{1,0:T(8,128)(2,1)S(1)}, bf16[128,384]{1,0:T(8,128)(2,1)}, u32[]{:S(2)}) copy-start(bf16[128,384]{1,0:T(8,128)(2,1)} %get-tuple-element.71) | copy-start | bytes 294916
  6.4 37.4 %copy-start.6 = (bf16[4,128,640]{2,1,0:T(8,128)(2,1)S(1)}, bf16[4,128,640]{2,1,0:T(8,128)(2,1)}, u32[]{:S(2)}) copy-start(bf16[4,128,640]{2,1,0:T(8,128)(2,1)} %get-tuple-element.75.refs_0_) | copy-start | bytes 1966084
  6.4 37.4 %copy-start.8 = (bf16[512,512]{1,0:T(8,128)(2,1)S(1)}, bf16[512,512]{1,0:T(8,128)(2,1)}, u32[]{:S(2)}) copy-start(bf16[512,512]{1,0:T(8,128)(2,1)} %constant.38.clone.refs_9_) | copy-start | bytes 1572868
  6.4 32.9 %collective-permute-start.1 = (bf16[4,128,640]{2,1,0:T(8,128)(2,1)}, bf16[4,128,640]{2,1,0:T(8,128)(2,1)S(1)}, u32[]{:S(2)}, u32[]{:S(2)}) collective-permute-start(bf16[4,128,640]{2,1,0:T(8,128)(2,1)} %get-tuple-element.64), channel_id=1, source_target_pairs={{0,2},{2,0},{4,6},{6,4},{1,3},{3,1},{5,7},{7,5},{8,10},{10,8},{12,... | collective-permute-start | bytes 1966088 | tf_op jit(solution)/shard_map/ppermute | solution.py:393
  9.5 29.8 %collective-permute-start.4 = (bf16[128,1024]{1,0:T(8,128)(2,1)}, bf16[128,1024]{1,0:T(8,128)(2,1)S(1)}, u32[]{:S(2)}, u32[]{:S(2)}) collective-permute-start(bf16[128,1024]{1,0:T(8,128)(2,1)} %get-tuple-element.67), channel_id=1, source_target_pairs={{0,4},{2,6},{4,0},{6,2},{1,5},{3,7},{5,1},{7,3},{8,12},{10,14},{12... | collective-permute-start | bytes 786440 | tf_op jit(solution)/shard_map/ppermute | solution.py:401
  12.1 22.0 %collective-permute-start.2 = (bf16[128,640]{1,0:T(8,128)(2,1)}, bf16[128,640]{1,0:T(8,128)(2,1)S(1)}, u32[]{:S(2)}, u32[]{:S(2)}) collective-permute-start(bf16[128,640]{1,0:T(8,128)(2,1)} %get-tuple-element.65), channel_id=1, source_target_pairs={{0,4},{2,6},{4,0},{6,2},{1,5},{3,7},{5,1},{7,3},{8,12},{10,14},{12... | collective-permute-start | bytes 491528 | tf_op jit(solution)/shard_map/ppermute | solution.py:396
  12.5 26.8 %collective-permute-start.3 = (bf16[128,640]{1,0:T(8,128)(2,1)}, bf16[128,640]{1,0:T(8,128)(2,1)S(1)}, u32[]{:S(2)}, u32[]{:S(2)}) collective-permute-start(bf16[128,640]{1,0:T(8,128)(2,1)} %get-tuple-element.66), channel_id=1, source_target_pairs={{0,6},{2,4},{4,2},{6,0},{1,7},{3,5},{5,3},{7,1},{8,14},{10,12},{12... | collective-permute-start | bytes 491528 | tf_op jit(solution)/shard_map/ppermute | solution.py:396
  39.3 4.5 %collective-permute-start.7 = (bf16[128,1024]{1,0:T(8,128)(2,1)S(1)}, bf16[128,1024]{1,0:T(8,128)(2,1)S(1)}, u32[]{:S(2)}, u32[]{:S(2)}) collective-permute-start(bf16[128,1024]{1,0:T(8,128)(2,1)S(1)} %collective-permute-done.4.refs_6_), channel_id=1, source_target_pairs={{0,8},{8,0},{16,24},{24,16},{1,9},{9,1},{17,25},{25,17},{2,10},{10... | collective-permute-start | bytes 786440 | tf_op jit(solution)/shard_map/ppermute | solution.py:417
  39.3 15.9 %copy-start.7 = (bf16[4,128,384]{2,1,0:T(8,128)(2,1)S(1)}, bf16[4,128,384]{2,1,0:T(8,128)(2,1)}, u32[]{:S(2)}) copy-start(bf16[4,128,384]{2,1,0:T(8,128)(2,1)} %get-tuple-element.59.refs_0_) | copy-start | bytes 1179652
  39.3 15.7 %collective-permute-start = (bf16[4,128,384]{2,1,0:T(8,128)(2,1)S(1)}, bf16[4,128,384]{2,1,0:T(8,128)(2,1)S(1)}, u32[]{:S(2)}, u32[]{:S(2)}) collective-permute-start(bf16[4,128,384]{2,1,0:T(8,128)(2,1)S(1)} %copy-done.9), channel_id=1, source_target_pairs={{0,2},{2,0},{4,6},{6,4},{1,3},{3,1},{5,7},{7,5},{8,10},{10,8},{12,... | collective-permute-start | bytes 1179656 | tf_op jit(solution)/shard_map/ppermute | solution.py:393
  39.4 15.6 %collective-permute-start.5 = (bf16[128,384]{1,0:T(8,128)(2,1)S(1)}, bf16[128,384]{1,0:T(8,128)(2,1)S(1)}, u32[]{:S(2)}, u32[]{:S(2)}) collective-permute-start(bf16[128,384]{1,0:T(8,128)(2,1)S(1)} %copy-done.11), channel_id=1, source_target_pairs={{0,4},{2,6},{4,0},{6,2},{1,5},{3,7},{5,1},{7,3},{8,12},{10,14},{12... | collective-permute-start | bytes 294920 | tf_op jit(solution)/shard_map/ppermute | solution.py:396
  41.5 13.7 %collective-permute-start.6 = (bf16[128,384]{1,0:T(8,128)(2,1)S(1)}, bf16[128,384]{1,0:T(8,128)(2,1)S(1)}, u32[]{:S(2)}, u32[]{:S(2)}) collective-permute-start(bf16[128,384]{1,0:T(8,128)(2,1)S(1)} %copy-done.10), channel_id=1, source_target_pairs={{0,6},{2,4},{4,2},{6,0},{1,7},{3,5},{5,3},{7,1},{8,14},{10,12},{12... | collective-permute-start | bytes 294920 | tf_op jit(solution)/shard_map/ppermute | solution.py:396
  51.3 14.3 %collective-permute-start.12 = (bf16[128,640]{1,0:T(8,128)(2,1)S(1)}, bf16[128,640]{1,0:T(8,128)(2,1)S(1)}, u32[]{:S(2)}, u32[]{:S(2)}) collective-permute-start(bf16[128,640]{1,0:T(8,128)(2,1)S(1)} %get-tuple-element.94), channel_id=1, source_target_pairs={{0,4},{2,6},{4,0},{6,2},{1,5},{3,7},{5,1},{7,3},{8,12},{10,14},{12... | collective-permute-start | bytes 491528 | tf_op jit(solution)/shard_map/ppermute | solution.py:396
  51.4 14.2 %collective-permute-start.13 = (bf16[128,640]{1,0:T(8,128)(2,1)S(1)}, bf16[128,640]{1,0:T(8,128)(2,1)S(1)}, u32[]{:S(2)}, u32[]{:S(2)}) collective-permute-start(bf16[128,640]{1,0:T(8,128)(2,1)S(1)} %get-tuple-element.95), channel_id=1, source_target_pairs={{0,6},{2,4},{4,2},{6,0},{1,7},{3,5},{5,3},{7,1},{8,14},{10,12},{12... | collective-permute-start | bytes 491528 | tf_op jit(solution)/shard_map/ppermute | solution.py:396
  55.0 32.2 %collective-permute-start.10 = (bf16[4,128,640]{2,1,0:T(8,128)(2,1)S(1)}, bf16[4,128,640]{2,1,0:T(8,128)(2,1)S(1)}, u32[]{:S(2)}, u32[]{:S(2)}) collective-permute-start(bf16[4,128,640]{2,1,0:T(8,128)(2,1)S(1)} %get-tuple-element.85), channel_id=1, source_target_pairs={{0,2},{2,0},{4,6},{6,4},{1,3},{3,1},{5,7},{7,5},{8,10},{10,8},{12,... | collective-permute-start | bytes 1966088 | tf_op jit(solution)/shard_map/ppermute | solution.py:393
  60.2 30.4 %copy-start = (bf16[128,4096]{1,0:T(8,128)(2,1)S(1)}, bf16[128,4096]{1,0:T(8,128)(2,1)}, u32[]{:S(2)}) copy-start(bf16[128,4096]{1,0:T(8,128)(2,1)} %refs_6_.5) | copy-start | bytes 3145732
  60.2 30.4 %copy-start.1 = (bf16[128,4096]{1,0:T(8,128)(2,1)S(1)}, bf16[128,4096]{1,0:T(8,128)(2,1)}, u32[]{:S(2)}) copy-start(bf16[128,4096]{1,0:T(8,128)(2,1)} %refs_5_.5) | copy-start | bytes 3145732
  60.2 30.4 %copy-start.2 = (bf16[128,4096]{1,0:T(8,128)(2,1)S(1)}, bf16[128,4096]{1,0:T(8,128)(2,1)}, u32[]{:S(2)}) copy-start(bf16[128,4096]{1,0:T(8,128)(2,1)} %refs_4_.5) | copy-start | bytes 3145732
  65.6 1.3 %collective-permute-start.16 = (bf16[384,128]{1,0:T(8,128)(2,1)S(1)}, bf16[384,128]{1,0:T(8,128)(2,1)S(1)}, u32[]{:S(2)}, u32[]{:S(2)}) collective-permute-start(bf16[384,128]{1,0:T(8,128)(2,1)S(1)} %get-tuple-element.107), channel_id=1, source_target_pairs={{0,8},{8,0},{16,24},{24,16},{1,9},{9,1},{17,25},{25,17},{2,10},{10... | collective-permute-start | bytes 294920 | tf_op jit(solution)/shard_map/ppermute | solution.py:359
  65.6 1.5 %collective-permute-start.18 = (bf16[384,128]{1,0:T(8,128)(2,1)S(1)}, bf16[384,128]{1,0:T(8,128)(2,1)S(1)}, u32[]{:S(2)}, u32[]{:S(2)}) collective-permute-start(bf16[384,128]{1,0:T(8,128)(2,1)S(1)} %get-tuple-element.109), channel_id=1, source_target_pairs={{0,8},{8,0},{16,24},{24,16},{1,9},{9,1},{17,25},{25,17},{2,10},{10... | collective-permute-start | bytes 294920 | tf_op jit(solution)/shard_map/ppermute | solution.py:359
  66.1 4.9 %collective-permute-start.14 = (bf16[384,256]{1,0:T(8,128)(2,1)S(1)}, bf16[384,256]{1,0:T(8,128)(2,1)S(1)}, u32[]{:S(2)}, u32[]{:S(2)}) collective-permute-start(bf16[384,256]{1,0:T(8,128)(2,1)S(1)} %get-tuple-element.105), channel_id=1, source_target_pairs={{0,8},{8,0},{16,24},{24,16},{1,9},{9,1},{17,25},{25,17},{2,10},{10... | collective-permute-start | bytes 589832 | tf_op jit(solution)/shard_map/ppermute | solution.py:359
  66.1 4.9 %collective-permute-start.15 = (bf16[384,256]{1,0:T(8,128)(2,1)S(1)}, bf16[384,256]{1,0:T(8,128)(2,1)S(1)}, u32[]{:S(2)}, u32[]{:S(2)}) collective-permute-start(bf16[384,256]{1,0:T(8,128)(2,1)S(1)} %get-tuple-element.106), channel_id=1, source_target_pairs={{0,8},{8,0},{16,24},{24,16},{1,9},{9,1},{17,25},{25,17},{2,10},{10... | collective-permute-start | bytes 589832 | tf_op jit(solution)/shard_map/ppermute | solution.py:359
  66.9 4.2 %collective-permute-start.17 = (bf16[384,256]{1,0:T(8,128)(2,1)S(1)}, bf16[384,256]{1,0:T(8,128)(2,1)S(1)}, u32[]{:S(2)}, u32[]{:S(2)}) collective-permute-start(bf16[384,256]{1,0:T(8,128)(2,1)S(1)} %get-tuple-element.108), channel_id=1, source_target_pairs={{0,8},{8,0},{16,24},{24,16},{1,9},{9,1},{17,25},{25,17},{2,10},{10... | collective-permute-start | bytes 589832 | tf_op jit(solution)/shard_map/ppermute | solution.py:359
  67.1 25.6 %collective-permute-start.8 = (bf16[4,128,384]{2,1,0:T(8,128)(2,1)S(1)}, bf16[4,128,384]{2,1,0:T(8,128)(2,1)S(1)}, u32[]{:S(2)}, u32[]{:S(2)}) collective-permute-start(bf16[4,128,384]{2,1,0:T(8,128)(2,1)S(1)} %get-tuple-element.81), channel_id=1, source_target_pairs={{0,2},{2,0},{4,6},{6,4},{1,3},{3,1},{5,7},{7,5},{8,10},{10,8},{12,... | collective-permute-start | bytes 1179656 | tf_op jit(solution)/shard_map/ppermute | solution.py:393
  71.3 17.1 %collective-permute-start.19 = (bf16[128,1024]{1,0:T(8,128)(2,1)S(1)}, bf16[128,1024]{1,0:T(8,128)(2,1)S(1)}, u32[]{:S(2)}, u32[]{:S(2)}) collective-permute-start(bf16[128,1024]{1,0:T(8,128)(2,1)S(1)} %get-tuple-element.111), channel_id=1, source_target_pairs={{0,4},{2,6},{4,0},{6,2},{1,5},{3,7},{5,1},{7,3},{8,12},{10,14},{12... | collective-permute-start | bytes 786440 | tf_op jit(solution)/shard_map/ppermute | solution.py:451
  73.4 19.3 %collective-permute-start.9 = (bf16[128,384]{1,0:T(8,128)(2,1)S(1)}, bf16[128,384]{1,0:T(8,128)(2,1)S(1)}, u32[]{:S(2)}, u32[]{:S(2)}) collective-permute-start(bf16[128,384]{1,0:T(8,128)(2,1)S(1)} %get-tuple-element.82), channel_id=1, source_target_pairs={{0,4},{2,6},{4,0},{6,2},{1,5},{3,7},{5,1},{7,3},{8,12},{10,14},{12... | collective-permute-start | bytes 294920 | tf_op jit(solution)/shard_map/ppermute | solution.py:396
  87.2 7.3 %collective-permute-start.11 = (bf16[128,384]{1,0:T(8,128)(2,1)S(1)}, bf16[128,384]{1,0:T(8,128)(2,1)S(1)}, u32[]{:S(2)}, u32[]{:S(2)}) collective-permute-start(bf16[128,384]{1,0:T(8,128)(2,1)S(1)} %get-tuple-element.86), channel_id=1, source_target_pairs={{0,6},{2,4},{4,2},{6,0},{1,7},{3,5},{5,3},{7,1},{8,14},{10,12},{12... | collective-permute-start | bytes 294920 | tf_op jit(solution)/shard_map/ppermute | solution.py:396
  89.0 7.8 %collective-permute-start.20 = (bf16[128,1024]{1,0:T(8,128)(2,1)S(1)}, bf16[128,1024]{1,0:T(8,128)(2,1)S(1)}, u32[]{:S(2)}, u32[]{:S(2)}) collective-permute-start(bf16[128,1024]{1,0:T(8,128)(2,1)S(1)} %get-tuple-element.113), channel_id=1, source_target_pairs={{0,16},{8,24},{16,0},{24,8},{1,17},{9,25},{17,1},{25,9},{2,18},{10... | collective-permute-start | bytes 786440 | tf_op jit(solution)/shard_map/ppermute | solution.py:465
where the time goes:
time: 97.8 us; the launch traced here: 97.7 us
  waiting for transfers between devices  44.8 us (46%)
  Pallas kernels  25.6 us (26%)
  starting transfers between devices  24.9 us (25%)
  other arithmetic  1.5 us (2%)
    ppermute x8, waiting for transfers between devices, pass_over(): lax.ppermute(x, 'seq', hop(half, 1, r))  28.4 us
    pallas_call x3, Pallas kernels, spectral(): pl.pallas_call(functools.partial(kernel, tile), in_specs=[pl.BlockSpec(me...  15.9 us
    ppermute x4, waiting for transfers between devices, pass_on(): lax.ppermute(x, 'seq', hop(half, 0, r))  14.8 us
    ppermute x8, starting transfers between devices, pass_over(): lax.ppermute(x, 'seq', hop(half, 1, r))  10.3 us
    ppermute x4, starting transfers between devices, pass_on(): lax.ppermute(x, 'seq', hop(half, 0, r))  7.15 us
    pallas_call x1, Pallas kernels, gate(): pl.pallas_call(functools.partial(gate_kernel, half, spans), grid_spec=plt...  5.07 us
    pallas_call x2, Pallas kernels, finish(): pl.pallas_call(functools.partial(finish_kernel, half, start), in_specs=[p...  3.79 us
    ppermute x1, starting transfers between devices, local(): near = lax.ppermute(near, 'seq', hop(half, 1, 0))  2.59 us
  transfers between devices with their start and end apart: 21, of which 10 were waited for; matrix products, arithmetic and copies ran while one was open for 0% of the time, Pallas kernels for 21%

commit v1 on v0

--- a/solution.py
+++ b/solution.py
@@ -52,66 +52,82 @@
     return lax.rem(place + half - steps, half)
 
 
+def position(half):
+    device = lax.axis_index("seq")
+    return device // half, device % half, lax.axis_index("dp")
+
+
 def group_of(info, place, other, half):
     side = 1 - info[0] if other else info[0]
     return side * half + place
 
 
-def gate_kernel(half, spans, info, *refs):
-    inputs, taps, outputs = refs[: 8 * half], refs[8 * half], refs[8 * half + 1 :]
+def gate_kernel(half, start, *refs):
+    outputs, held, sems = refs[5 - bool(start) : 5 - bool(start) + 2 * half], refs[-2], refs[-1]
+    info = position(half)
     lower = info[0] == 0
-    outputs[-1][...] = taps[...].astype(jnp.bfloat16)
-    for r in range(half):
-        for t in (0, 1):
-            query, key, value, grad = (
-                ref[...].astype(jnp.float32) for ref in inputs[8 * r + 4 * t : 8 * r + 4 * t + 4]
-            )
-            mixed, scaled = key * value, grad * query
-            first = jnp.where(lower, mixed, scaled).astype(jnp.bfloat16)
-            second = jnp.where(lower, scaled, mixed).astype(jnp.bfloat16)
-            for chunk, cols in enumerate(spans):
-                outputs[chunk * 2 * half + r][t] = first[:, cols]
-                outputs[chunk * 2 * half + r][2 + t] = second[:, cols]
-                if t:
-                    outputs[chunk * 2 * half + half + r][...] = first[:, cols]
-
-
-def gate(info, half, spans, rows, taps):
+    block, width = held.shape[2:]
+    group = refs[0].shape[1] // (2 * half)
+    copies = []
+    for s in range(2 * half):
+        col = group_of(info, after(info[1], s // 2, half), s % 2, half) * group + start
+        cols = pl.ds(pl.multiple_of(col, 128), width)
+        for i, row in enumerate(refs[:4]):
+            copies.append(pltpu.make_async_copy(row.at[:, cols], held.at[i, s], sems.at[i, s]))
+            copies[-1].start()
+    if not start:
+        taps, held_taps, taps_sem = refs[4], refs[-4], refs[-3]
+        piece = held_taps.shape[0]
+        mine = pl.ds(pl.multiple_of(info[2] % 2 * piece, piece), piece)
+        taps_copy = pltpu.make_async_copy(taps.at[mine, :], held_taps, taps_sem)
+        taps_copy.start()
+    for s in range(2 * half):
+        for copy in copies[4 * s : 4 * s + 4]:
+            copy.wait()
+        r, t = s // 2, s % 2
+        pair, cross = outputs[r], outputs[half + r]
+        query, key, value, grad = (held[i, s].astype(jnp.float32) for i in range(4))
+        mixed, scaled = key * value, grad * query
+        first = jnp.where(lower, mixed, scaled).astype(jnp.bfloat16)
+        pair[t] = first
+        pair[2 + t] = jnp.where(lower, scaled, mixed).astype(jnp.bfloat16)
+        if t and (start or r):
+            cross[...] = first
+        elif t:
+            for j in range(width // 128):
+                cross[j * block : (j + 1) * block, :] = first[:, j * 128 : (j + 1) * 128]
+    if not start:
+        taps_copy.wait()
+        base = width // 128 * block
+        for j in range(group // 128):
+            part = held_taps[:, j * 128 : (j + 1) * 128].astype(jnp.bfloat16)
+            outputs[half][base + j * piece : base + (j + 1) * piece, :] = part
+
+
+def gate(half, cols, rows, taps):
     tokens, channels = rows[0].shape
     group = channels // (2 * half)
-    piece = taps.shape[0] // 4
-
-    def column(i, info, r, t):
-        return (0, group_of(info, after(info[1], r, half), t, half))
-
-    in_specs = [
-        pl.BlockSpec((tokens, group), functools.partial(column, r=r, t=t))
-        for r in range(half)
-        for t in (0, 1)
-        for _ in range(4)
+    width, piece = cols.stop - cols.start, taps.shape[0] // 4
+    shapes = [(4, tokens, width)] * half + [(tokens, width)] * half
+    scratch = [
+        pltpu.VMEM((4, 2 * half, tokens, width), jnp.bfloat16),
+        pltpu.SemaphoreType.DMA((4, 2 * half)),
     ]
-    in_specs.append(pl.BlockSpec((piece, group), lambda i, info: (info[2] % 2, 0)))
-    shapes = []
-    for cols in spans:
-        width = cols.stop - cols.start
-        shapes += [(4, tokens, width)] * half + [(tokens, width)] * half
-    shapes.append((piece, group))
+    operands = list(rows)
+    if not cols.start:
+        shapes[half] = ((width * tokens + group * piece) // 128, 128)
+        scratch = [pltpu.VMEM((piece, group), jnp.float32), pltpu.SemaphoreType.DMA] + scratch
+        operands.append(taps)
     outs = pl.pallas_call(
-        functools.partial(gate_kernel, half, spans),
-        grid_spec=pltpu.PrefetchScalarGridSpec(
-            num_scalar_prefetch=1,
-            grid=(1,),
-            in_specs=in_specs,
-            out_specs=[
-                pl.BlockSpec(s, lambda i, info, n=len(s): (0,) * n) for s in shapes
-            ],
-        ),
+        functools.partial(gate_kernel, half, cols.start),
+        in_specs=[pl.BlockSpec(memory_space=pl.ANY)] * len(operands),
+        out_specs=[pl.BlockSpec(memory_space=pltpu.VMEM)] * len(shapes),
         out_shape=[jax.ShapeDtypeStruct(s, jnp.bfloat16) for s in shapes],
+        scratch_shapes=scratch,
         compiler_params=pltpu.CompilerParams(vmem_limit_bytes=56 << 20),
         cost_estimate=tiny,
-    )(info, *(list(rows) * (2 * half)), taps)
-    parts = [outs[2 * half * c : 2 * half * (c + 1)] for c in range(len(spans))]
-    return [x[:half] for x in parts], [x[half:] for x in parts], outs[-1]
+    )(*operands)
+    return outs[:half], outs[half:]
 
 
 def high_low(x):
@@ -193,7 +209,7 @@
             ref[row + i * lags : row + (i + 1) * lags, cols] = part.astype(ref.dtype)
 
 
-def taps_kernel(tile, info, taps, fwd, near_spec, all_spec, high, low):
+def taps_kernel(tile, taps, fwd, near_spec, all_spec, high, low):
     length = taps.shape[0] // 2
     matrix = chosen(fwd, 0)
     for cols in tiles(taps.shape[1], tile):
@@ -212,13 +228,14 @@
         by_strips(length, tile, body)
 
 
-def conv_kernel(half, replicas, start, tile, info, *refs):
+def conv_kernel(half, replicas, start, tile, *refs):
     pairs, crosses, refs = refs[:half], refs[half : 2 * half], refs[2 * half :]
-    tap_spec, tap_all, *near, fwd, inv = refs[:6]
+    tap_spec, tap_all, first_cross, near, fwd, inv = refs[:6]
     refs = refs[7 if start else 6 :]
     pair_outs, cross_outs, keep = refs[:half], refs[half : 2 * half], refs[2 * half]
     *sends, data, near_all, spec, near_spec, high, conv, grads = refs[2 * half + 1 :]
-    side, place, core = info[0], info[1], info[2] % 2
+    side, place, replica = position(half)
+    core = replica % 2
     _, block, width = pairs[0].shape
     length = half * block
     piece = length // 2
@@ -228,10 +245,19 @@
         whole = slice(start + cols.start, start + cols.stop)
         for j in range(4):
             place_rows(data, j, [pair.at[j] for pair in pairs], cols, place, half)
-        place_rows(data, 4, crosses, cols, place, half)
-        for j in (0, 1):
-            rows = pl.ds(pl.multiple_of((core ^ j) * piece, piece), piece)
-            near_all[rows, :wide] = near[j][:, whole]
+        if start:
+            place_rows(data, 4, crosses, cols, place, half)
+        for j in range(0 if start else wide // 128):
+            k = cols.start // 128 + j
+            parts = [crosses[0].at[k * block : (k + 1) * block]]
+            parts += [cross.at[:, k * 128 : (k + 1) * 128] for cross in crosses[1:]]
+            place_rows(data, 4 * wide // 128 + j, parts, slice(0, 128), place, half)
+        for mine, source in ((core, first_cross), (1 - core, near)):
+            rows = pl.ds(pl.multiple_of(mine * piece, piece), piece)
+            base = source.shape[0] - near.shape[0]
+            for j in range(wide // 128):
+                k = base + (whole.start // 128 + j) * piece
+                near_all[rows, j * 128 : (j + 1) * 128] = source[k : k + piece, :]
         spec[:, : 5 * wide] = transform(fwd_data, data[:, : 5 * wide])
         near_spec[:, :wide] = transform(chosen(fwd, 0), near_all[:, :wide])
 
@@ -265,25 +291,26 @@
     return [slice(i, min(i + tile, width)) for i in range(0, width, tile)]
 
 
-def spectral(kernel, tile, info, operands, shapes, scratch, cost, aliases={}):
+def spectral(kernel, tile, operands, shapes, scratch, cost, aliases={}):
     tile = min(tile, shapes[0][0][-1])
     vmem = pl.BlockSpec(memory_space=pltpu.VMEM)
     return pl.pallas_call(
         functools.partial(kernel, tile),
-        in_specs=[pl.BlockSpec(memory_space=pltpu.SMEM)] + [vmem] * len(operands),
+        in_specs=[vmem] * len(operands),
         out_specs=[vmem] * len(shapes),
         scratch_shapes=[pltpu.VMEM((r, n * tile), t) for r, n, t in scratch],
         out_shape=[jax.ShapeDtypeStruct(s, t) for s, t in shapes],
         compiler_params=pltpu.CompilerParams(vmem_limit_bytes=VMEM),
         input_output_aliases=aliases,
         cost_estimate=cost,
-    )(info, *operands)
-
-
-def finish_kernel(half, start, info, *refs):
+    )(*operands)
+
+
+def finish_kernel(half, start, *refs):
     received = refs[: 2 * half]
     grad, value, key = refs[2 * half : 2 * half + 3]
     *outs, made, sems = refs[-5:]
+    info = position(half)
     lower = info[0] == 0
     width = made.shape[3]
     group = grad.shape[1] // (2 * half)
@@ -308,24 +335,22 @@
         copy.wait()
 
 
-def finish(info, half, start, pairs, crosses, grad, value, key, earlier):
+def finish(half, start, pairs, crosses, grad, value, key, earlier):
     tokens, width = crosses[0].shape
     vmem, anywhere = pl.BlockSpec(memory_space=pltpu.VMEM), pl.BlockSpec(memory_space=pl.ANY)
     return pl.pallas_call(
         functools.partial(finish_kernel, half, start),
-        in_specs=[pl.BlockSpec(memory_space=pltpu.SMEM)]
-        + [vmem] * (2 * half + 3)
-        + [anywhere] * len(earlier),
+        in_specs=[vmem] * (2 * half + 3) + [anywhere] * len(earlier),
         out_specs=[anywhere] * 3,
         out_shape=[jax.ShapeDtypeStruct(grad.shape, jnp.bfloat16)] * 3,
         scratch_shapes=[
             pltpu.VMEM((3, 2 * half, tokens, width), jnp.bfloat16),
             pltpu.SemaphoreType.DMA((3, 2 * half)),
         ],
-        input_output_aliases={2 * half + 4 + i: i for i in range(len(earlier))},
+        input_output_aliases={2 * half + 3 + i: i for i in range(len(earlier))},
         compiler_params=pltpu.CompilerParams(vmem_limit_bytes=VMEM),
         cost_estimate=large if earlier else tiny,
-    )(info, *pairs, *crosses, grad, value, key, *earlier)
+    )(*pairs, *crosses, grad, value, key, *earlier)
 
 
 def sum_kernel(keep, *refs):
@@ -335,59 +360,76 @@
     for send in sends:
         cols = slice(start, start + send.shape[1])
         start = cols.stop
-        own[:, cols] = keep[:rows, cols] + send[:rows, :].astype(jnp.float32)
-        total = keep[rows:, cols] + send[rows:, :].astype(jnp.float32)
-        other[:, cols] = total.astype(other.dtype)
-
-
-def last_kernel(bit, info, own, over, go, stay):
-    upper = info[2] & bit != 0
-    first, second = own[0] + over[...].astype(jnp.float32), own[1]
+        total = keep[:, cols] + send[...].astype(jnp.float32)
+        own[:, cols] = total[:rows]
+        other[:, cols] = total[rows:].astype(other.dtype)
+
+
+def last_kernel(bit, own, over, stay, go):
+    upper = lax.axis_index("dp") & bit != 0
+    lags = over.shape[0]
+    first, second = own[:lags] + over[...].astype(jnp.float32), own[lags:]
+    stay[...] = jnp.where(upper, second, first)
     go[...] = jnp.where(upper, first, second).astype(go.dtype)
-    stay[...] = jnp.where(upper, second, first)
-
-
-def halve(x, bit, replicas, wire):
+
+
+def add_kernel(stay, arrived, out):
+    out[...] = stay[...] + arrived[...].astype(jnp.float32)
+
+
+def halve(x, bit):
     upper = lax.axis_index("dp") & bit != 0
     x = x.reshape(-1, 2, *x.shape[1:])
-    go = jnp.where(upper, x[:, 0], x[:, 1]).astype(wire)
-    stay = jnp.where(upper, x[:, 1], x[:, 0])
-    return stay + lax.ppermute(go, "dp", flip(replicas, bit)).astype(jnp.float32)
-
-
-def sum_lags(keep, sends, length, replicas):
-    sends = [lax.ppermute(x, "dp", flip(replicas, 1)) for x in sends]
+    return jnp.where(upper, x[:, 1], x[:, 0]), jnp.where(upper, x[:, 0], x[:, 1])
+
+
+def in_vmem(kernel, operands, shapes):
     vmem = pl.BlockSpec(memory_space=pltpu.VMEM)
-    width = keep.shape[1]
-    own, other = pl.pallas_call(
-        sum_kernel,
-        in_specs=[vmem] * (1 + len(sends)),
-        out_specs=[vmem, vmem],
-        out_shape=[
-            jax.ShapeDtypeStruct((length, width), jnp.float32),
-            jax.ShapeDtypeStruct(
-                (length // 2, width), jnp.bfloat16 if replicas == 4 else jnp.float32
-            ),
-        ],
+    return pl.pallas_call(
+        kernel,
+        in_specs=[vmem] * len(operands),
+        out_specs=[vmem] * len(shapes),
+        out_shape=[jax.ShapeDtypeStruct(s, t) for s, t in shapes],
         compiler_params=pltpu.CompilerParams(vmem_limit_bytes=VMEM),
         cost_estimate=tiny,
-    )(keep, *sends)
-    lags = 2 * length // replicas
-    own, other = own.reshape(-1, lags, width), other.reshape(-1, lags, width)
+    )(*operands)
+
+
+def sum_filter(keep, sends, length, half, replicas):
+    f32, bf16 = jnp.float32, jnp.bfloat16
+    lags, width = 2 * length // replicas, keep.shape[1]
+    sends = [lax.ppermute(x, "dp", flip(replicas, 1)) for x in sends]
+    own, other = in_vmem(
+        sum_kernel,
+        [keep, *sends],
+        [((length, width), f32), ((length // 2, width), bf16 if replicas == 4 else f32)],
+    )
     bit = 2
     while bit < replicas // 2:
-        own, other = (halve(x, bit, replicas, jnp.float32) for x in (own, other))
+        own, other = (
+            stay + lax.ppermute(go, "dp", flip(replicas, bit))
+            for stay, go in (halve(x.reshape(-1, lags, width), bit) for x in (own, other))
+        )
         bit *= 2
-    return own, other[0].astype(jnp.bfloat16)
+    own, other = own.reshape(-1, width), other.reshape(-1, width).astype(bf16)
+    over = lax.ppermute(other, "seq", hop(half, 1, 0))
+    stay, go = in_vmem(
+        functools.partial(last_kernel, bit),
+        [own, over],
+        [((lags, width), f32), ((lags, width), bf16)],
+    )
+    arrived = lax.ppermute(go, "dp", flip(replicas, bit))
+    return in_vmem(add_kernel, [stay, arrived], [(stay.shape, f32)])[0]
 
 
 def local(replicas, half, query, key, value, grad, taps):
-    place = lax.axis_index("seq")
-    info = jnp.stack([place // half, place % half, lax.axis_index("dp")]).astype(jnp.int32)
     length, width = taps.shape[0] // 2, taps.shape[1]
     block = query.shape[0]
     f32, bf16 = jnp.float32, jnp.bfloat16
     forward, inverse = (jnp.asarray(t) for t in tables(length))
+    cut = width * 5 // 8 // 128 * 128
+    cut = cut or width
+    spans = [slice(0, cut), slice(cut, width)] if cut < width else [slice(0, width)]
 
     def pass_on(pairs):
         return [lax.ppermute(x, "seq", hop(half, 0, r)) if r else x for r, x in enumerate(pairs)]
@@ -395,34 +437,33 @@
     def pass_over(crosses):
         return [lax.ppermute(x, "seq", hop(half, 1, r)) for r, x in enumerate(crosses)]
 
-    cut = width * 5 // 8 // 128 * 128
-    spans = [slice(0, cut), slice(cut, width)] if cut else [slice(0, width)]
-    pairs, crosses, near = gate(info, half, spans, (query, key, value, grad), taps)
-    near = lax.ppermute(near, "seq", hop(half, 1, 0))
+    def tie(*parts):
+        return lax.optimization_barrier(parts)
+
+    gated = [gate(half, cols, (query, key, value, grad), taps) for cols in spans]
+    pairs, crosses = [list(x) for x in zip(*gated, strict=True)]
     tap_specs = spectral(
         taps_kernel,
         256,
-        info,
         [taps, forward],
         [((2 * length, width), f32)] * 2,
         [(length, 2, bf16), (length, 2, bf16)],
         tiny,
     )
-    pairs, crosses[0] = [pass_on(x) for x in pairs], pass_over(crosses[0])
+    pairs[0], crosses[0] = pass_on(pairs[0]), pass_over(crosses[0])
     for c in range(1, len(spans)):
-        crosses[c], (pairs[0], crosses[0], near, tap_specs) = lax.optimization_barrier(
-            (crosses[c], (pairs[0], crosses[0], near, tap_specs))
+        pairs[c], crosses[c], pairs[0], crosses[0], tap_specs = tie(
+            pairs[c], crosses[c], pairs[0], crosses[0], tap_specs
         )
-        crosses[c] = pass_over(crosses[c])
-    near = (near, lax.ppermute(near, "dp", flip(replicas, 1)))
+        pairs[c], crosses[c] = pass_on(pairs[c]), pass_over(crosses[c])
+    near = lax.ppermute(crosses[0][0][cut * block // 128 :], "dp", flip(replicas, 1))
     results, cross_results, keep, sends = [], [], [], []
     for c, cols in enumerate(spans):
         wide = cols.stop - cols.start
         outs = spectral(
             functools.partial(conv_kernel, half, replicas, cols.start),
             256,
-            info,
-            [*pairs[c], *crosses[c], *tap_specs, *near, forward, inverse, *keep],
+            [*pairs[c], *crosses[c], *tap_specs, crosses[0][0], near, forward, inverse, *keep],
             [((4, block, wide), bf16)] * half
             + [((block, wide), bf16)] * half
             + [((3 * length // 2, width), f32)]
@@ -437,32 +478,19 @@
                 (length, 3, f32),
             ],
             large,
-            {2 * half + 7: 2 * half} if c else {},
+            {2 * half + 6: 2 * half} if c else {},
         )
         keep, *more = outs[2 * half :]
         keep, sends = [keep], sends + more
         cross = list(outs[half : 2 * half])
         if c:
-            sends, cross_results[-1] = lax.optimization_barrier((sends, cross_results[-1]))
-            cross[-1], results[-1] = lax.optimization_barrier((cross[-1], results[-1]))
+            sends, cross_results[-1] = tie(sends, cross_results[-1])
         results.append(pass_on(outs[:half]))
         cross_results.append(pass_over(cross))
-    own, other = sum_lags(*keep, sends, length, replicas)
-    other = lax.ppermute(other, "seq", hop(half, 1, 0))
+    grad_filter = sum_filter(*keep, sends, length, half, replicas)
     outs = []
     for c, cols in enumerate(spans):
-        outs = finish(info, half, cols.start, results[c], cross_results[c], grad, value, key, outs)
-    vmem = pl.BlockSpec(memory_space=pltpu.VMEM)
-    bit = replicas // 2
-    go, stay = pl.pallas_call(
-        functools.partial(last_kernel, bit),
-        in_specs=[pl.BlockSpec(memory_space=pltpu.SMEM), vmem, vmem],
-        out_specs=[vmem, vmem],
-        out_shape=[jax.ShapeDtypeStruct(other.shape, t) for t in (bf16, f32)],
-        compiler_params=pltpu.CompilerParams(vmem_limit_bytes=VMEM),
-        cost_estimate=tiny,
-    )(info, own, other)
-    grad_filter = stay + lax.ppermute(go, "dp", flip(replicas, bit)).astype(f32)
+        outs = finish(half, cols.start, results[c], cross_results[c], grad, value, key, outs)
     return *outs, grad_filter
 
 

time: 97.8 us -> 95.6 us (0.978)
  waiting for transfers between devices: 44.8 us -> 49.1 us
  starting transfers between devices: 24.9 us -> 21.3 us
  Pallas kernels: 25.6 us -> 24.1 us
  other arithmetic: 1.5 us -> 0 us
    ppermute x9 -> x8, waiting for transfers between devices: 1.64 us -> 13.7 us  [the longest x1 12.1 us: sum_filter(): over = lax.ppermute(other, 'seq', hop(half, 1, 0))]
    ppermute x8, waiting for transfers between devices: 28.4 us -> 24.4 us  [pass_over(): lax.ppermute(x, 'seq', hop(half, 1, r))]
    ppermute x4, waiting for transfers between devices: 14.8 us -> 11.1 us  [pass_on(): lax.ppermute(x, 'seq', hop(half, 0, r))]
    ppermute x9 -> x8, starting transfers between devices: 7.42 us -> 4.89 us  [the longest x1 2.02 us: sum_filter(): over = lax.ppermute(other, 'seq', hop(half, 1, 0))]
    pallas_call x8 -> x10, Pallas kernels: 25.6 us -> 24.1 us  [the longest x3 14.1 us: spectral(): pl.pallas_call(functools.partial(kernel, tile), in_specs=[vmem] * len(ope...]
    ppermute x4, starting transfers between devices: 7.15 us -> 5.86 us  [pass_on(): lax.ppermute(x, 'seq', hop(half, 0, r))]
  transfers between devices with their start and end apart: 21 -> 20, of which waited for: 10 -> 9; matrix products, arithmetic and copies ran while one was open for 0% -> 0% of each run, Pallas kernels for 21% -> 21%
where the time goes in v1:
time: 95.6 us; the launch traced here: 95.5 us
  waiting for transfers between devices  49.1 us (51%)
  Pallas kernels  24.1 us (25%)
  starting transfers between devices  21.3 us (22%)
    ppermute x8, waiting for transfers between devices, pass_over(): lax.ppermute(x, 'seq', hop(half, 1, r))  24.4 us
    pallas_call x3, Pallas kernels, spectral(): pl.pallas_call(functools.partial(kernel, tile), in_specs=[vmem] * len(ope...  14.1 us
    ppermute x1, waiting for transfers between devices, sum_filter(): over = lax.ppermute(other, 'seq', hop(half, 1, 0))  12.1 us
    ppermute x4, waiting for transfers between devices, pass_on(): lax.ppermute(x, 'seq', hop(half, 0, r))  11.1 us
    ppermute x8, starting transfers between devices, pass_over(): lax.ppermute(x, 'seq', hop(half, 1, r))  10.6 us
    pallas_call x2, Pallas kernels, gate(): pl.pallas_call(functools.partial(gate_kernel, half, cols.start), in_specs...  6.1 us
    ppermute x4, starting transfers between devices, pass_on(): lax.ppermute(x, 'seq', hop(half, 0, r))  5.86 us
    pallas_call x2, Pallas kernels, finish(): pl.pallas_call(functools.partial(finish_kernel, half, start), in_specs=[v...  2.73 us
  transfers between devices with their start and end apart: 20, of which 9 were waited for; matrix products, arithmetic and copies ran while one was open for 0% of the time, Pallas kernels for 21%

profile of v1, /device:TPU:0, one launch (start us, length us, event | category | flops | bytes accessed | tf_op | source)
XLA Modules:
  0.0 95.5 jit_solution(14898918508351000957)
XLA Ops:
  0.6 3.4 %shard_map.103 = (bf16[4,128,640]{2,1,0:T(8,128)(2,1)}, bf16[4,128,640]{2,1,0:T(8,128)(2,1)}, bf16[1664,128]{1,0:T(8,128)(2,1)}, bf16[128,640]{1,0:T(8,128)(2,1)}) custom-call(bf16[128,4096]{1,0:T(8,128)(2,1)} %refs_0_.3, bf16[128,4096]{1,0:T(8,128)(2,1)} %refs_6_.3, bf16[128,4096]{1,0:T(8,128)(2,1)} %refs_5_.3, bf16[128,4096]{1,0:T(8,128)(2,1)} %refs_4_.5, ...), custom_call_target="tpu_custom_call" | custom-call | bytes 1 | tf_op jit(solution)/shard_map/pallas_call | solution.py:121
  4.0 3.1 %collective-permute-start = (bf16[4,128,640]{2,1,0:T(8,128)(2,1)}, bf16[4,128,640]{2,1,0:T(8,128)(2,1)S(1)}, u32[]{:S(2)}, u32[]{:S(2)}) collective-permute-start(bf16[4,128,640]{2,1,0:T(8,128)(2,1)} %get-tuple-element.61), channel_id=1, source_target_pairs={{0,2},{2,0},{4,6},{6,4},{1,3},{3,1},{5,7},{7,5},{8,10},{10,8},{12,... | collective-permute-start | bytes 1966088 | tf_op jit(solution)/shard_map/ppermute | solution.py:435
  7.1 2.6 %collective-permute-start.1 = (bf16[1664,128]{1,0:T(8,128)(2,1)}, bf16[1664,128]{1,0:T(8,128)(2,1)S(1)}, u32[]{:S(2)}, u32[]{:S(2)}) collective-permute-start(bf16[1664,128]{1,0:T(8,128)(2,1)} %get-tuple-element.62), channel_id=1, source_target_pairs={{0,4},{2,6},{4,0},{6,2},{1,5},{3,7},{5,1},{7,3},{8,12},{10,14},{12... | collective-permute-start | bytes 1277960 | tf_op jit(solution)/shard_map/ppermute | solution.py:438
  9.7 0.0 collective-permute-start.2
  9.7 2.7 %shard_map.102 = (bf16[4,128,384]{2,1,0:T(8,128)(2,1)}, bf16[4,128,384]{2,1,0:T(8,128)(2,1)}, bf16[128,384]{1,0:T(8,128)(2,1)}, bf16[128,384]{1,0:T(8,128)(2,1)}) custom-call(bf16[128,4096]{1,0:T(8,128)(2,1)} %refs_0_.3, bf16[128,4096]{1,0:T(8,128)(2,1)} %refs_6_.3, bf16[128,4096]{1,0:T(8,128)(2,1)} %refs_5_.3, bf16[128,4096]{1,0:T(8,128)(2,1)} %refs_4_.5), custom_call_target="tpu_custom_call" | custom-call | bytes 1 | tf_op jit(solution)/shard_map/pallas_call | solution.py:121
  12.5 0.0 copy-start.5
  12.5 0.0 copy-start.7
  12.5 2.8 %shard_map.104 = (f32[512,1024]{1,0:T(8,128)S(1)}, f32[512,1024]{1,0:T(8,128)S(1)}) custom-call(f32[512,1024]{1,0:T(8,128)S(1)} %copy-done.3, bf16[2048,256]{1,0:T(8,128)(2,1)S(1)} %copy-done.4), custom_call_target="tpu_custom_call" | custom-call | bytes 1 | tf_op jit(solution)/shard_map/pallas_call | solution.py:297
  15.3 21.6 %collective-permute-done.2.refs_3_ = bf16[128,640]{1,0:T(8,128)(2,1)S(1)} collective-permute-done((bf16[128,640]{1,0:T(8,128)(2,1)}, bf16[128,640]{1,0:T(8,128)(2,1)S(1)}, u32[]{:S(2)}, u32[]{:S(2)}) %collective-permute-start.2) | collective-permute-done | bytes 163872 | tf_op jit(solution)/shard_map/ppermute | solution.py:438
  36.9 0.0 copy-start.6
  36.9 0.1 collective-permute-start.6
  37.0 0.1 collective-permute-start.4
  37.1 1.6 %collective-permute-start.5 = (bf16[128,384]{1,0:T(8,128)(2,1)S(1)}, bf16[128,384]{1,0:T(8,128)(2,1)S(1)}, u32[]{:S(2)}, u32[]{:S(2)}) collective-permute-start(bf16[128,384]{1,0:T(8,128)(2,1)S(1)} %copy-done.9), channel_id=1, source_target_pairs={{0,6},{2,4},{4,2},{6,0},{1,7},{3,5},{5,3},{7,1},{8,14},{10,12},{12... | collective-permute-start | bytes 294920 | tf_op jit(solution)/shard_map/ppermute | solution.py:438
  38.8 1.8 %collective-permute-start.3 = (bf16[4,128,384]{2,1,0:T(8,128)(2,1)S(1)}, bf16[4,128,384]{2,1,0:T(8,128)(2,1)S(1)}, u32[]{:S(2)}, u32[]{:S(2)}) collective-permute-start(bf16[4,128,384]{2,1,0:T(8,128)(2,1)S(1)} %copy-done.8), channel_id=1, source_target_pairs={{0,2},{2,0},{4,6},{6,4},{1,3},{3,1},{5,7},{7,5},{8,10},{10,8},{12,... | collective-permute-start | bytes 1179656 | tf_op jit(solution)/shard_map/ppermute | solution.py:435
  40.6 6.9 %shard_map.105 = (bf16[4,128,640]{2,1,0:T(8,128)(2,1)S(1)}, bf16[4,128,640]{2,1,0:T(8,128)(2,1)S(1)}, bf16[128,640]{1,0:T(8,128)(2,1)S(1)}, bf16[128,640]{1,0:T(...) custom-call(bf16[4,128,640]{2,1,0:T(8,128)(2,1)S(1)} %copy-done.5, ...), custom_call_target="tpu_custom_call" | custom-call | flops 34359738368 | bytes 1 | tf_op jit(solution)/shard_map/pallas_call | solution.py:297
  47.5 1.1 %collective-permute-start.11 = (bf16[128,640]{1,0:T(8,128)(2,1)S(1)}, bf16[128,640]{1,0:T(8,128)(2,1)S(1)}, u32[]{:S(2)}, u32[]{:S(2)}) collective-permute-start(bf16[128,640]{1,0:T(8,128)(2,1)S(1)} %get-tuple-element.88), channel_id=1, source_target_pairs={{0,4},{2,6},{4,0},{6,2},{1,5},{3,7},{5,1},{7,3},{8,12},{10,14},{12... | collective-permute-start | bytes 491528 | tf_op jit(solution)/shard_map/ppermute | solution.py:438
  48.6 1.6 %collective-permute-start.12 = (bf16[128,640]{1,0:T(8,128)(2,1)S(1)}, bf16[128,640]{1,0:T(8,128)(2,1)S(1)}, u32[]{:S(2)}, u32[]{:S(2)}) collective-permute-start(bf16[128,640]{1,0:T(8,128)(2,1)S(1)} %get-tuple-element.89), channel_id=1, source_target_pairs={{0,6},{2,4},{4,2},{6,0},{1,7},{3,5},{5,3},{7,1},{8,14},{10,12},{12... | collective-permute-start | bytes 491528 | tf_op jit(solution)/shard_map/ppermute | solution.py:438
  50.2 0.9 collective-permute-start.10
  51.1 0.0 collective-permute-done.5.refs_3_
  51.1 9.8 %collective-permute-done.3.refs_1_ = bf16[4,128,384]{2,1,0:T(8,128)(2,1)S(1)} collective-permute-done((bf16[4,128,384]{2,1,0:T(8,128)(2,1)S(1)}, bf16[4,128,384]{2,1,0:T(8,128)(2,1)S(1)}, u32[]{:S(2)}, u32[]{:S(2)}) %collective-permute-start.3) | collective-permute-done | bytes 393248 | tf_op jit(solution)/shard_map/ppermute | solution.py:435
  60.9 4.4 %shard_map.106 = (bf16[4,128,384]{2,1,0:T(8,128)(2,1)S(1)}, bf16[4,128,384]{2,1,0:T(8,128)(2,1)S(1)}, bf16[128,384]{1,0:T(8,128)(2,1)S(1)}, bf16[128,384]{1,0:T(...) custom-call(bf16[4,128,384]{2,1,0:T(8,128)(2,1)S(1)} %copy-done.6, ...), custom_call_target="tpu_custom_call", output_to_operand_aliasing={{4}: (10, {})} | custom-call | flops 34359738368 | bytes 1 | tf_op jit(solution)/shard_map/pallas_call | solution.py:297
  65.3 0.0 copy-start
  65.3 0.0 copy-start.1
  65.3 0.0 copy-start.2
  65.3 0.0 collective-permute-done.11.refs_2_
  65.3 0.0 collective-permute-done.12.refs_3_
  65.3 0.1 collective-permute-start.15
  65.4 0.5 collective-permute-start.17
  65.9 0.1 collective-permute-start.13
  66.0 0.4 collective-permute-start.14
  66.4 0.3 collective-permute-done.15.refs_2_
  66.7 0.2 collective-permute-start.16
  66.8 0.0 collective-permute-start.7
  66.9 0.5 collective-permute-done.13.refs_0_
  67.3 0.3 collective-permute-done.14.refs_1_
  67.6 0.5 collective-permute-done.16.refs_3_
  68.1 0.2 shard_map.109
  68.3 2.0 %collective-permute-start.18 = (bf16[128,1024]{1,0:T(8,128)(2,1)S(1)}, bf16[128,1024]{1,0:T(8,128)(2,1)S(1)}, u32[]{:S(2)}, u32[]{:S(2)}) collective-permute-start(bf16[128,1024]{1,0:T(8,128)(2,1)S(1)} %get-tuple-element.105), channel_id=1, source_target_pairs={{0,4},{2,6},{4,0},{6,2},{1,5},{3,7},{5,1},{7,3},{8,12},{10,14},{12... | collective-permute-start | bytes 786440 | tf_op jit(solution)/shard_map/ppermute | solution.py:415
  70.4 1.0 %collective-permute-start.8 = (bf16[128,384]{1,0:T(8,128)(2,1)S(1)}, bf16[128,384]{1,0:T(8,128)(2,1)S(1)}, u32[]{:S(2)}, u32[]{:S(2)}) collective-permute-start(bf16[128,384]{1,0:T(8,128)(2,1)S(1)} %get-tuple-element.79), channel_id=1, source_target_pairs={{0,4},{2,6},{4,0},{6,2},{1,5},{3,7},{5,1},{7,3},{8,12},{10,14},{12... | collective-permute-start | bytes 294920 | tf_op jit(solution)/shard_map/ppermute | solution.py:438
  71.3 2.6 %collective-permute-start.9 = (bf16[128,384]{1,0:T(8,128)(2,1)S(1)}, bf16[128,384]{1,0:T(8,128)(2,1)S(1)}, u32[]{:S(2)}, u32[]{:S(2)}) collective-permute-start(bf16[128,384]{1,0:T(8,128)(2,1)S(1)} %get-tuple-element.80), channel_id=1, source_target_pairs={{0,6},{2,4},{4,2},{6,0},{1,7},{3,5},{5,3},{7,1},{8,14},{10,12},{12... | collective-permute-start | bytes 294920 | tf_op jit(solution)/shard_map/ppermute | solution.py:438
  74.0 12.1 %collective-permute-done.18.over = bf16[128,1024]{1,0:T(8,128)(2,1)S(1)} collective-permute-done((bf16[128,1024]{1,0:T(8,128)(2,1)S(1)}, bf16[128,1024]{1,0:T(8,128)(2,1)S(1)}, u32[]{:S(2)}, u32[]{:S(2)}) %collective-permute-start.18) | collective-permute-done | bytes 262176 | tf_op jit(solution)/shard_map/ppermute | solution.py:415
  86.1 0.1 shard_map.110
  86.2 1.6 %collective-permute-start.19 = (bf16[128,1024]{1,0:T(8,128)(2,1)S(1)}, bf16[128,1024]{1,0:T(8,128)(2,1)S(1)}, u32[]{:S(2)}, u32[]{:S(2)}) collective-permute-start(bf16[128,1024]{1,0:T(8,128)(2,1)S(1)} %get-tuple-element.107), channel_id=1, source_target_pairs={{0,16},{8,24},{16,0},{24,8},{1,17},{9,25},{17,1},{25,9},{2,18},{10... | collective-permute-start | bytes 786440 | tf_op jit(solution)/shard_map/ppermute | solution.py:421
  87.8 1.5 %shard_map.107 = (bf16[128,4096]{1,0:T(8,128)(2,1)}, bf16[128,4096]{1,0:T(8,128)(2,1)}, bf16[128,4096]{1,0:T(8,128)(2,1)}) custom-call(bf16[4,128,640]{2,1,0:T(8,128)(2,1)S(1)} %get-tuple-element.81.refs_0_, bf16[4,128,640]{2,1,0:T(8,128)(2,1)S(1)} %collective-permute-done.10.refs_1_, bf16[128,640]{1,0:T(8,128)(2,1)S(1)} %collective-permute-done.11.refs_2_, ...), custom_call_target="tpu_custom_call" | custom-call | bytes 1 | tf_op jit(solution)/shard_map/pallas_call | solution.py:341
  89.4 2.8 %collective-permute-done.9.refs_3_ = bf16[128,384]{1,0:T(8,128)(2,1)S(1)} collective-permute-done((bf16[128,384]{1,0:T(8,128)(2,1)S(1)}, bf16[128,384]{1,0:T(8,128)(2,1)S(1)}, u32[]{:S(2)}, u32[]{:S(2)}) %collective-permute-start.9) | collective-permute-done | bytes 98336 | tf_op jit(solution)/shard_map/ppermute | solution.py:438
  92.1 1.3 %collective-permute-done.7.refs_1_ = bf16[4,128,384]{2,1,0:T(8,128)(2,1)S(1)} collective-permute-done((bf16[4,128,384]{2,1,0:T(8,128)(2,1)S(1)}, bf16[4,128,384]{2,1,0:T(8,128)(2,1)S(1)}, u32[]{:S(2)}, u32[]{:S(2)}) %collective-permute-start.7) | collective-permute-done | bytes 393248 | tf_op jit(solution)/shard_map/ppermute | solution.py:435
  93.4 1.2 %shard_map.108 = (bf16[128,4096]{1,0:T(8,128)(2,1)}, bf16[128,4096]{1,0:T(8,128)(2,1)}, bf16[128,4096]{1,0:T(8,128)(2,1)}) custom-call(bf16[4,128,384]{2,1,0:T(8,128)(2,1)S(1)} %get-tuple-element.77.refs_0_, bf16[4,128,384]{2,1,0:T(8,128)(2,1)S(1)} %collective-permute-done.7.refs_1_, ...), custom_call_target="tpu_custom_call", output_to_operand_aliasing={{0}: (7, {}), {1}: (8, {}), {2}: (9, {})} | custom-call | flops 34359738368 | bytes 1 | tf_op jit(solution)/shard_map/pallas_call | solution.py:341
  94.6 0.8 shard_map.111
  (25 shorter events, 0.1 us)
Async XLA Ops:
  4.0 32.9 %collective-permute-start = (bf16[4,128,640]{2,1,0:T(8,128)(2,1)}, bf16[4,128,640]{2,1,0:T(8,128)(2,1)S(1)}, u32[]{:S(2)}, u32[]{:S(2)}) collective-permute-start(bf16[4,128,640]{2,1,0:T(8,128)(2,1)} %get-tuple-element.61), channel_id=1, source_target_pairs={{0,2},{2,0},{4,6},{6,4},{1,3},{3,1},{5,7},{7,5},{8,10},{10,8},{12,... | collective-permute-start | bytes 1966088 | tf_op jit(solution)/shard_map/ppermute | solution.py:435
  7.1 29.8 %collective-permute-start.1 = (bf16[1664,128]{1,0:T(8,128)(2,1)}, bf16[1664,128]{1,0:T(8,128)(2,1)S(1)}, u32[]{:S(2)}, u32[]{:S(2)}) collective-permute-start(bf16[1664,128]{1,0:T(8,128)(2,1)} %get-tuple-element.62), channel_id=1, source_target_pairs={{0,4},{2,6},{4,0},{6,2},{1,5},{3,7},{5,1},{7,3},{8,12},{10,14},{12... | collective-permute-start | bytes 1277960 | tf_op jit(solution)/shard_map/ppermute | solution.py:438
  9.7 2.7 %copy-start.3 = (f32[512,1024]{1,0:T(8,128)S(1)}, f32[512,1024]{1,0:T(8,128)}, u32[]{:S(2)}) copy-start(f32[512,1024]{1,0:T(8,128)} %taps.1) | copy-start | bytes 6291460
  9.7 2.7 %copy-start.4 = (bf16[2048,256]{1,0:T(8,128)(2,1)S(1)}, bf16[2048,256]{1,0:T(8,128)(2,1)}, u32[]{:S(2)}) copy-start(bf16[2048,256]{1,0:T(8,128)(2,1)} %constant.4.clone.fwd.refs_8_) | copy-start | bytes 3145732
  9.7 27.2 %collective-permute-start.2 = (bf16[128,640]{1,0:T(8,128)(2,1)}, bf16[128,640]{1,0:T(8,128)(2,1)S(1)}, u32[]{:S(2)}, u32[]{:S(2)}) collective-permute-start(bf16[128,640]{1,0:T(8,128)(2,1)} %get-tuple-element.63), channel_id=1, source_target_pairs={{0,6},{2,4},{4,2},{6,0},{1,7},{3,5},{5,3},{7,1},{8,14},{10,12},{12... | collective-permute-start | bytes 491528 | tf_op jit(solution)/shard_map/ppermute | solution.py:438
  12.4 24.6 %copy-start.10 = (bf16[128,384]{1,0:T(8,128)(2,1)S(1)}, bf16[128,384]{1,0:T(8,128)(2,1)}, u32[]{:S(2)}) copy-start(bf16[128,384]{1,0:T(8,128)(2,1)} %get-tuple-element.68) | copy-start | bytes 294916
  12.5 24.7 %copy-start.9 = (bf16[128,384]{1,0:T(8,128)(2,1)S(1)}, bf16[128,384]{1,0:T(8,128)(2,1)}, u32[]{:S(2)}) copy-start(bf16[128,384]{1,0:T(8,128)(2,1)} %get-tuple-element.69) | copy-start | bytes 294916
  12.5 26.3 %copy-start.8 = (bf16[4,128,384]{2,1,0:T(8,128)(2,1)S(1)}, bf16[4,128,384]{2,1,0:T(8,128)(2,1)}, u32[]{:S(2)}) copy-start(bf16[4,128,384]{2,1,0:T(8,128)(2,1)} %get-tuple-element.67) | copy-start | bytes 1179652
  12.5 28.1 %copy-start.5 = (bf16[4,128,640]{2,1,0:T(8,128)(2,1)S(1)}, bf16[4,128,640]{2,1,0:T(8,128)(2,1)}, u32[]{:S(2)}) copy-start(bf16[4,128,640]{2,1,0:T(8,128)(2,1)} %get-tuple-element.73.refs_0_) | copy-start | bytes 1966084
  12.5 28.1 %copy-start.7 = (bf16[512,512]{1,0:T(8,128)(2,1)S(1)}, bf16[512,512]{1,0:T(8,128)(2,1)}, u32[]{:S(2)}) copy-start(bf16[512,512]{1,0:T(8,128)(2,1)} %constant.5.clone.refs_9_) | copy-start | bytes 1572868
  36.9 23.9 %copy-start.6 = (bf16[4,128,384]{2,1,0:T(8,128)(2,1)S(1)}, bf16[4,128,384]{2,1,0:T(8,128)(2,1)}, u32[]{:S(2)}) copy-start(bf16[4,128,384]{2,1,0:T(8,128)(2,1)} %get-tuple-element.66.refs_0_) | copy-start | bytes 1179652
  36.9 3.7 %collective-permute-start.6 = (bf16[1024,128]{1,0:T(8,128)(2,1)S(1)}, bf16[1024,128]{1,0:T(8,128)(2,1)S(1)}, u32[]{:S(2)}, u32[]{:S(2)}) collective-permute-start(bf16[1024,128]{1,0:T(8,128)(2,1)S(1)} %slice.3), channel_id=1, source_target_pairs={{0,8},{8,0},{16,24},{24,16},{1,9},{9,1},{17,25},{25,17},{2,10},{10... | collective-permute-start | bytes 786440 | tf_op jit(solution)/shard_map/ppermute | solution.py:459
  37.0 13.1 %collective-permute-start.4 = (bf16[128,384]{1,0:T(8,128)(2,1)S(1)}, bf16[128,384]{1,0:T(8,128)(2,1)S(1)}, u32[]{:S(2)}, u32[]{:S(2)}) collective-permute-start(bf16[128,384]{1,0:T(8,128)(2,1)S(1)} %copy-done.10), channel_id=1, source_target_pairs={{0,4},{2,6},{4,0},{6,2},{1,5},{3,7},{5,1},{7,3},{8,12},{10,14},{12... | collective-permute-start | bytes 294920 | tf_op jit(solution)/shard_map/ppermute | solution.py:438
  37.1 14.0 %collective-permute-start.5 = (bf16[128,384]{1,0:T(8,128)(2,1)S(1)}, bf16[128,384]{1,0:T(8,128)(2,1)S(1)}, u32[]{:S(2)}, u32[]{:S(2)}) collective-permute-start(bf16[128,384]{1,0:T(8,128)(2,1)S(1)} %copy-done.9), channel_id=1, source_target_pairs={{0,6},{2,4},{4,2},{6,0},{1,7},{3,5},{5,3},{7,1},{8,14},{10,12},{12... | collective-permute-start | bytes 294920 | tf_op jit(solution)/shard_map/ppermute | solution.py:438
  38.8 22.1 %collective-permute-start.3 = (bf16[4,128,384]{2,1,0:T(8,128)(2,1)S(1)}, bf16[4,128,384]{2,1,0:T(8,128)(2,1)S(1)}, u32[]{:S(2)}, u32[]{:S(2)}) collective-permute-start(bf16[4,128,384]{2,1,0:T(8,128)(2,1)S(1)} %copy-done.8), channel_id=1, source_target_pairs={{0,2},{2,0},{4,6},{6,4},{1,3},{3,1},{5,7},{7,5},{8,10},{10,8},{12,... | collective-permute-start | bytes 1179656 | tf_op jit(solution)/shard_map/ppermute | solution.py:435
  47.5 17.8 %collective-permute-start.11 = (bf16[128,640]{1,0:T(8,128)(2,1)S(1)}, bf16[128,640]{1,0:T(8,128)(2,1)S(1)}, u32[]{:S(2)}, u32[]{:S(2)}) collective-permute-start(bf16[128,640]{1,0:T(8,128)(2,1)S(1)} %get-tuple-element.88), channel_id=1, source_target_pairs={{0,4},{2,6},{4,0},{6,2},{1,5},{3,7},{5,1},{7,3},{8,12},{10,14},{12... | collective-permute-start | bytes 491528 | tf_op jit(solution)/shard_map/ppermute | solution.py:438
  48.6 16.7 %collective-permute-start.12 = (bf16[128,640]{1,0:T(8,128)(2,1)S(1)}, bf16[128,640]{1,0:T(8,128)(2,1)S(1)}, u32[]{:S(2)}, u32[]{:S(2)}) collective-permute-start(bf16[128,640]{1,0:T(8,128)(2,1)S(1)} %get-tuple-element.89), channel_id=1, source_target_pairs={{0,6},{2,4},{4,2},{6,0},{1,7},{3,5},{5,3},{7,1},{8,14},{10,12},{12... | collective-permute-start | bytes 491528 | tf_op jit(solution)/shard_map/ppermute | solution.py:438
  50.2 37.6 %collective-permute-start.10 = (bf16[4,128,640]{2,1,0:T(8,128)(2,1)S(1)}, bf16[4,128,640]{2,1,0:T(8,128)(2,1)S(1)}, u32[]{:S(2)}, u32[]{:S(2)}) collective-permute-start(bf16[4,128,640]{2,1,0:T(8,128)(2,1)S(1)} %get-tuple-element.82), channel_id=1, source_target_pairs={{0,2},{2,0},{4,6},{6,4},{1,3},{3,1},{5,7},{7,5},{8,10},{10,8},{12,... | collective-permute-start | bytes 1966088 | tf_op jit(solution)/shard_map/ppermute | solution.py:435
  65.3 22.5 %copy-start = (bf16[128,4096]{1,0:T(8,128)(2,1)S(1)}, bf16[128,4096]{1,0:T(8,128)(2,1)}, u32[]{:S(2)}) copy-start(bf16[128,4096]{1,0:T(8,128)(2,1)} %refs_6_.3) | copy-start | bytes 3145732
  65.3 22.5 %copy-start.1 = (bf16[128,4096]{1,0:T(8,128)(2,1)S(1)}, bf16[128,4096]{1,0:T(8,128)(2,1)}, u32[]{:S(2)}) copy-start(bf16[128,4096]{1,0:T(8,128)(2,1)} %refs_5_.3) | copy-start | bytes 3145732
  65.3 22.5 %copy-start.2 = (bf16[128,4096]{1,0:T(8,128)(2,1)S(1)}, bf16[128,4096]{1,0:T(8,128)(2,1)}, u32[]{:S(2)}) copy-start(bf16[128,4096]{1,0:T(8,128)(2,1)} %refs_4_.5) | copy-start | bytes 3145732
  65.3 1.4 %collective-permute-start.15 = (bf16[384,128]{1,0:T(8,128)(2,1)S(1)}, bf16[384,128]{1,0:T(8,128)(2,1)S(1)}, u32[]{:S(2)}, u32[]{:S(2)}) collective-permute-start(bf16[384,128]{1,0:T(8,128)(2,1)S(1)} %get-tuple-element.101), channel_id=1, source_target_pairs={{0,8},{8,0},{16,24},{24,16},{1,9},{9,1},{17,25},{25,17},{2,10},{10... | collective-permute-start | bytes 294920 | tf_op jit(solution)/shard_map/ppermute | solution.py:401
  65.4 1.4 %collective-permute-start.17 = (bf16[384,128]{1,0:T(8,128)(2,1)S(1)}, bf16[384,128]{1,0:T(8,128)(2,1)S(1)}, u32[]{:S(2)}, u32[]{:S(2)}) collective-permute-start(bf16[384,128]{1,0:T(8,128)(2,1)S(1)} %get-tuple-element.103), channel_id=1, source_target_pairs={{0,8},{8,0},{16,24},{24,16},{1,9},{9,1},{17,25},{25,17},{2,10},{10... | collective-permute-start | bytes 294920 | tf_op jit(solution)/shard_map/ppermute | solution.py:401
  65.9 1.4 %collective-permute-start.13 = (bf16[384,256]{1,0:T(8,128)(2,1)S(1)}, bf16[384,256]{1,0:T(8,128)(2,1)S(1)}, u32[]{:S(2)}, u32[]{:S(2)}) collective-permute-start(bf16[384,256]{1,0:T(8,128)(2,1)S(1)} %get-tuple-element.99), channel_id=1, source_target_pairs={{0,8},{8,0},{16,24},{24,16},{1,9},{9,1},{17,25},{25,17},{2,10},{10... | collective-permute-start | bytes 589832 | tf_op jit(solution)/shard_map/ppermute | solution.py:401
  66.0 1.6 %collective-permute-start.14 = (bf16[384,256]{1,0:T(8,128)(2,1)S(1)}, bf16[384,256]{1,0:T(8,128)(2,1)S(1)}, u32[]{:S(2)}, u32[]{:S(2)}) collective-permute-start(bf16[384,256]{1,0:T(8,128)(2,1)S(1)} %get-tuple-element.100), channel_id=1, source_target_pairs={{0,8},{8,0},{16,24},{24,16},{1,9},{9,1},{17,25},{25,17},{2,10},{10... | collective-permute-start | bytes 589832 | tf_op jit(solution)/shard_map/ppermute | solution.py:401
  66.7 1.4 %collective-permute-start.16 = (bf16[384,256]{1,0:T(8,128)(2,1)S(1)}, bf16[384,256]{1,0:T(8,128)(2,1)S(1)}, u32[]{:S(2)}, u32[]{:S(2)}) collective-permute-start(bf16[384,256]{1,0:T(8,128)(2,1)S(1)} %get-tuple-element.102), channel_id=1, source_target_pairs={{0,8},{8,0},{16,24},{24,16},{1,9},{9,1},{17,25},{25,17},{2,10},{10... | collective-permute-start | bytes 589832 | tf_op jit(solution)/shard_map/ppermute | solution.py:401
  66.8 26.6 %collective-permute-start.7 = (bf16[4,128,384]{2,1,0:T(8,128)(2,1)S(1)}, bf16[4,128,384]{2,1,0:T(8,128)(2,1)S(1)}, u32[]{:S(2)}, u32[]{:S(2)}) collective-permute-start(bf16[4,128,384]{2,1,0:T(8,128)(2,1)S(1)} %get-tuple-element.78), channel_id=1, source_target_pairs={{0,2},{2,0},{4,6},{6,4},{1,3},{3,1},{5,7},{7,5},{8,10},{10,8},{12,... | collective-permute-start | bytes 1179656 | tf_op jit(solution)/shard_map/ppermute | solution.py:435
  68.3 17.8 %collective-permute-start.18 = (bf16[128,1024]{1,0:T(8,128)(2,1)S(1)}, bf16[128,1024]{1,0:T(8,128)(2,1)S(1)}, u32[]{:S(2)}, u32[]{:S(2)}) collective-permute-start(bf16[128,1024]{1,0:T(8,128)(2,1)S(1)} %get-tuple-element.105), channel_id=1, source_target_pairs={{0,4},{2,6},{4,0},{6,2},{1,5},{3,7},{5,1},{7,3},{8,12},{10,14},{12... | collective-permute-start | bytes 786440 | tf_op jit(solution)/shard_map/ppermute | solution.py:415
  70.4 19.0 %collective-permute-start.8 = (bf16[128,384]{1,0:T(8,128)(2,1)S(1)}, bf16[128,384]{1,0:T(8,128)(2,1)S(1)}, u32[]{:S(2)}, u32[]{:S(2)}) collective-permute-start(bf16[128,384]{1,0:T(8,128)(2,1)S(1)} %get-tuple-element.79), channel_id=1, source_target_pairs={{0,4},{2,6},{4,0},{6,2},{1,5},{3,7},{5,1},{7,3},{8,12},{10,14},{12... | collective-permute-start | bytes 294920 | tf_op jit(solution)/shard_map/ppermute | solution.py:438
  71.3 20.8 %collective-permute-start.9 = (bf16[128,384]{1,0:T(8,128)(2,1)S(1)}, bf16[128,384]{1,0:T(8,128)(2,1)S(1)}, u32[]{:S(2)}, u32[]{:S(2)}) collective-permute-start(bf16[128,384]{1,0:T(8,128)(2,1)S(1)} %get-tuple-element.80), channel_id=1, source_target_pairs={{0,6},{2,4},{4,2},{6,0},{1,7},{3,5},{5,3},{7,1},{8,14},{10,12},{12... | collective-permute-start | bytes 294920 | tf_op jit(solution)/shard_map/ppermute | solution.py:438
  86.2 8.4 %collective-permute-start.19 = (bf16[128,1024]{1,0:T(8,128)(2,1)S(1)}, bf16[128,1024]{1,0:T(8,128)(2,1)S(1)}, u32[]{:S(2)}, u32[]{:S(2)}) collective-permute-start(bf16[128,1024]{1,0:T(8,128)(2,1)S(1)} %get-tuple-element.107), channel_id=1, source_target_pairs={{0,16},{8,24},{16,0},{24,8},{1,17},{9,25},{17,1},{25,9},{2,18},{10... | collective-permute-start | bytes 786440 | tf_op jit(solution)/shard_map/ppermute | solution.py:421

commit v2 on v1

--- a/solution.py
+++ b/solution.py
@@ -353,28 +353,45 @@
     )(*pairs, *crosses, grad, value, key, *earlier)
 
 
-def sum_kernel(keep, *refs):
-    *sends, own, other = refs
+def sum_kernel(replicas, keep, *refs):
+    *sends, own, stay, go = refs
     rows = own.shape[0]
+    upper = lax.axis_index("dp") & (replicas // 2) != 0
     start = 0
     for send in sends:
         cols = slice(start, start + send.shape[1])
         start = cols.stop
         total = keep[:, cols] + send[...].astype(jnp.float32)
         own[:, cols] = total[:rows]
-        other[:, cols] = total[rows:].astype(other.dtype)
+        if replicas == 4:
+            lags = (total.shape[0] - rows) // 2
+            first, second = total[rows : rows + lags], total[rows + lags :]
+            stay[:, cols] = jnp.where(upper, second, first)
+            go[:, cols] = jnp.where(upper, first, second).astype(go.dtype)
+        else:
+            stay[:, cols] = total[rows:]
+            go[:, cols] = jnp.zeros_like(go[:, cols])
+
+
+def over_kernel(stay, arrived, out):
+    out[...] = (stay[...] + arrived[...].astype(jnp.float32)).astype(out.dtype)
+
+
+def add_kernel(stay, arrived, out):
+    out[...] = stay[...] + arrived[...].astype(jnp.float32)
 
 
 def last_kernel(bit, own, over, stay, go):
     upper = lax.axis_index("dp") & bit != 0
-    lags = over.shape[0]
-    first, second = own[:lags] + over[...].astype(jnp.float32), own[lags:]
-    stay[...] = jnp.where(upper, second, first)
-    go[...] = jnp.where(upper, first, second).astype(go.dtype)
-
-
-def add_kernel(stay, arrived, out):
-    out[...] = stay[...] + arrived[...].astype(jnp.float32)
+    lags, part = own.shape[0] // 2, over.shape[0]
+    added = over[...].astype(jnp.float32)
+    zeros = jnp.zeros_like(added)
+    for i in (0, 1):
+        rows = slice(i * part, (i + 1) * part)
+        first = own[rows] + jnp.where(upper == bool(i), added, zeros)
+        second = own[lags + i * part : lags + (i + 1) * part]
+        stay[rows] = jnp.where(upper, second, first)
+        go[rows] = jnp.where(upper, first, second).astype(go.dtype)
 
 
 def halve(x, bit):
@@ -399,19 +416,29 @@
     f32, bf16 = jnp.float32, jnp.bfloat16
     lags, width = 2 * length // replicas, keep.shape[1]
     sends = [lax.ppermute(x, "dp", flip(replicas, 1)) for x in sends]
-    own, other = in_vmem(
-        sum_kernel,
+    once = replicas == 4
+    own, stay, go = in_vmem(
+        functools.partial(sum_kernel, replicas),
         [keep, *sends],
-        [((length, width), f32), ((length // 2, width), bf16 if replicas == 4 else f32)],
+        [
+            ((length, width), f32),
+            ((lags // 2 if once else length // 2, width), f32),
+            ((lags // 2, width), bf16),
+        ],
     )
     bit = 2
-    while bit < replicas // 2:
-        own, other = (
-            stay + lax.ppermute(go, "dp", flip(replicas, bit))
-            for stay, go in (halve(x.reshape(-1, lags, width), bit) for x in (own, other))
-        )
-        bit *= 2
-    own, other = own.reshape(-1, width), other.reshape(-1, width).astype(bf16)
+    if not once:
+        own, other = own.reshape(-1, lags, width), stay.reshape(-1, lags, width)
+        while bit < replicas // 2:
+            own, other = (
+                stay + lax.ppermute(go, "dp", flip(replicas, bit))
+                for stay, go in (halve(x, bit) for x in (own, other))
+            )
+            bit *= 2
+        stay, go = (x[0] for x in halve(other.reshape(2, lags // 2, width), bit))
+        own, go = own.reshape(-1, width), go.astype(bf16)
+    arrived = lax.ppermute(go, "dp", flip(replicas, bit))
+    (other,) = in_vmem(over_kernel, [stay, arrived], [(stay.shape, bf16)])
     over = lax.ppermute(other, "seq", hop(half, 1, 0))
     stay, go = in_vmem(
         functools.partial(last_kernel, bit),
@@ -452,8 +479,8 @@
     )
     pairs[0], crosses[0] = pass_on(pairs[0]), pass_over(crosses[0])
     for c in range(1, len(spans)):
-        pairs[c], crosses[c], pairs[0], crosses[0], tap_specs = tie(
-            pairs[c], crosses[c], pairs[0], crosses[0], tap_specs
+        crosses[c], pairs[0], crosses[0], tap_specs = tie(
+            crosses[c], pairs[0], crosses[0], tap_specs
         )
         pairs[c], crosses[c] = pass_on(pairs[c]), pass_over(crosses[c])
     near = lax.ppermute(crosses[0][0][cut * block // 128 :], "dp", flip(replicas, 1))
@@ -477,7 +504,7 @@
                 (length, 5, bf16),
                 (length, 3, f32),
             ],
-            large,
+            large if c else tiny,
             {2 * half + 6: 2 * half} if c else {},
         )
         keep, *more = outs[2 * half :]

time: 95.6 us -> 90.9 us (0.951)
  waiting for transfers between devices: 49.1 us -> 40.1 us
  starting transfers between devices: 21.3 us -> 25.6 us
    ppermute x4, waiting for transfers between devices: 11.1 us -> 0.01 us  [pass_on(): lax.ppermute(x, 'seq', hop(half, 0, r))]
    ppermute x1, waiting for transfers between devices: 12.1 us -> 4.54 us  [sum_filter(): over = lax.ppermute(other, 'seq', hop(half, 1, 0))]
    ppermute x8, waiting for transfers between devices: 24.4 us -> 31.3 us  [pass_over(): lax.ppermute(x, 'seq', hop(half, 1, r))]
    ppermute x1 -> x2, waiting for transfers between devices: 0.01 us -> 3.95 us  [sum_filter(): arrived = lax.ppermute(go, 'dp', flip(replicas, bit))]
    ppermute x4, starting transfers between devices: 5.86 us -> 7.49 us  [pass_on(): lax.ppermute(x, 'seq', hop(half, 0, r))]
    ppermute x1 -> x2, starting transfers between devices: 1.57 us -> 3.15 us  [sum_filter(): arrived = lax.ppermute(go, 'dp', flip(replicas, bit))]
    ppermute x5, waiting for transfers between devices: 1.54 us -> 0.29 us  [sum_filter(): sends = [lax.ppermute(x, 'dp', flip(replicas, 1)) for x in sends]]
    ppermute x8, starting transfers between devices: 10.6 us -> 11.6 us  [pass_over(): lax.ppermute(x, 'seq', hop(half, 1, r))]
  transfers between devices with their start and end apart: 20 -> 21, of which waited for: 9 -> 6; matrix products, arithmetic and copies ran while one was open for 0% -> 0% of each run, Pallas kernels for 21% -> 22%
where the time goes in v2:
time: 90.9 us; the launch traced here: 90.8 us
  waiting for transfers between devices  40.1 us (44%)
  starting transfers between devices  25.6 us (28%)
  Pallas kernels  24.2 us (27%)
    ppermute x8, waiting for transfers between devices, pass_over(): lax.ppermute(x, 'seq', hop(half, 1, r))  31.3 us
    pallas_call x3, Pallas kernels, spectral(): pl.pallas_call(functools.partial(kernel, tile), in_specs=[vmem] * len(ope...  14.1 us
    ppermute x8, starting transfers between devices, pass_over(): lax.ppermute(x, 'seq', hop(half, 1, r))  11.6 us
    ppermute x4, starting transfers between devices, pass_on(): lax.ppermute(x, 'seq', hop(half, 0, r))  7.49 us
    pallas_call x2, Pallas kernels, gate(): pl.pallas_call(functools.partial(gate_kernel, half, cols.start), in_specs...  6.1 us
    ppermute x1, waiting for transfers between devices, sum_filter(): over = lax.ppermute(other, 'seq', hop(half, 1, 0))  4.54 us
    ppermute x2, waiting for transfers between devices, sum_filter(): arrived = lax.ppermute(go, 'dp', flip(replicas, bit))  3.95 us
    ppermute x2, starting transfers between devices, sum_filter(): arrived = lax.ppermute(go, 'dp', flip(replicas, bit))  3.15 us
  transfers between devices with their start and end apart: 21, of which 6 were waited for; matrix products, arithmetic and copies ran while one was open for 0% of the time, Pallas kernels for 22%

profile of v2, /device:TPU:0, one launch (start us, length us, event | category | flops | bytes accessed | tf_op | source)
XLA Modules:
  0.0 90.8 jit_solution(13362128945584834235)
XLA Ops:
  0.6 3.4 %shard_map.103 = (bf16[4,128,640]{2,1,0:T(8,128)(2,1)}, bf16[4,128,640]{2,1,0:T(8,128)(2,1)}, bf16[1664,128]{1,0:T(8,128)(2,1)}, bf16[128,640]{1,0:T(8,128)(2,1)}) custom-call(bf16[128,4096]{1,0:T(8,128)(2,1)} %refs_0_.3, bf16[128,4096]{1,0:T(8,128)(2,1)} %refs_6_.3, bf16[128,4096]{1,0:T(8,128)(2,1)} %refs_5_.3, bf16[128,4096]{1,0:T(8,128)(2,1)} %refs_4_.5, ...), custom_call_target="tpu_custom_call" | custom-call | bytes 1 | tf_op jit(solution)/shard_map/pallas_call | solution.py:121
  4.0 3.1 %collective-permute-start.1 = (bf16[4,128,640]{2,1,0:T(8,128)(2,1)}, bf16[4,128,640]{2,1,0:T(8,128)(2,1)S(1)}, u32[]{:S(2)}, u32[]{:S(2)}) collective-permute-start(bf16[4,128,640]{2,1,0:T(8,128)(2,1)} %get-tuple-element.60), channel_id=1, source_target_pairs={{0,2},{2,0},{4,6},{6,4},{1,3},{3,1},{5,7},{7,5},{8,10},{10,8},{12,... | collective-permute-start | bytes 1966088 | tf_op jit(solution)/shard_map/ppermute | solution.py:462
  7.1 2.6 %collective-permute-start.2 = (bf16[1664,128]{1,0:T(8,128)(2,1)}, bf16[1664,128]{1,0:T(8,128)(2,1)S(1)}, u32[]{:S(2)}, u32[]{:S(2)}) collective-permute-start(bf16[1664,128]{1,0:T(8,128)(2,1)} %get-tuple-element.61), channel_id=1, source_target_pairs={{0,4},{2,6},{4,0},{6,2},{1,5},{3,7},{5,1},{7,3},{8,12},{10,14},{12... | collective-permute-start | bytes 1277960 | tf_op jit(solution)/shard_map/ppermute | solution.py:465
  9.7 0.0 collective-permute-start.3
  9.7 2.7 %shard_map.102 = (bf16[4,128,384]{2,1,0:T(8,128)(2,1)}, bf16[4,128,384]{2,1,0:T(8,128)(2,1)}, bf16[128,384]{1,0:T(8,128)(2,1)}, bf16[128,384]{1,0:T(8,128)(2,1)}) custom-call(bf16[128,4096]{1,0:T(8,128)(2,1)} %refs_0_.3, bf16[128,4096]{1,0:T(8,128)(2,1)} %refs_6_.3, bf16[128,4096]{1,0:T(8,128)(2,1)} %refs_5_.3, bf16[128,4096]{1,0:T(8,128)(2,1)} %refs_4_.5), custom_call_target="tpu_custom_call" | custom-call | bytes 1 | tf_op jit(solution)/shard_map/pallas_call | solution.py:121
  12.4 0.0 copy-start.5
  12.5 0.0 copy-start.6
  12.5 1.0 %collective-permute-start = (bf16[4,128,384]{2,1,0:T(8,128)(2,1)}, bf16[4,128,384]{2,1,0:T(8,128)(2,1)S(1)}, u32[]{:S(2)}, u32[]{:S(2)}) collective-permute-start(bf16[4,128,384]{2,1,0:T(8,128)(2,1)} %get-tuple-element.56), channel_id=1, source_target_pairs={{0,2},{2,0},{4,6},{6,4},{1,3},{3,1},{5,7},{7,5},{8,10},{10,8},{12,... | collective-permute-start | bytes 1179656 | tf_op jit(solution)/shard_map/ppermute | solution.py:462
  13.5 2.8 %shard_map.104 = (f32[512,1024]{1,0:T(8,128)S(1)}, f32[512,1024]{1,0:T(8,128)S(1)}) custom-call(f32[512,1024]{1,0:T(8,128)S(1)} %copy-done.3, bf16[2048,256]{1,0:T(8,128)(2,1)S(1)} %copy-done.4), custom_call_target="tpu_custom_call" | custom-call | bytes 1 | tf_op jit(solution)/shard_map/pallas_call | solution.py:297
  16.3 21.8 %collective-permute-done.3.refs_3_ = bf16[128,640]{1,0:T(8,128)(2,1)S(1)} collective-permute-done((bf16[128,640]{1,0:T(8,128)(2,1)}, bf16[128,640]{1,0:T(8,128)(2,1)S(1)}, u32[]{:S(2)}, u32[]{:S(2)}) %collective-permute-start.3) | collective-permute-done | bytes 163872 | tf_op jit(solution)/shard_map/ppermute | solution.py:465
  38.1 0.0 copy-start.7
  38.1 0.1 collective-permute-start.6
  38.2 0.1 collective-permute-start.4
  38.3 1.6 %collective-permute-start.5 = (bf16[128,384]{1,0:T(8,128)(2,1)S(1)}, bf16[128,384]{1,0:T(8,128)(2,1)S(1)}, u32[]{:S(2)}, u32[]{:S(2)}) collective-permute-start(bf16[128,384]{1,0:T(8,128)(2,1)S(1)} %copy-done.8), channel_id=1, source_target_pairs={{0,6},{2,4},{4,2},{6,0},{1,7},{3,5},{5,3},{7,1},{8,14},{10,12},{12... | collective-permute-start | bytes 294920 | tf_op jit(solution)/shard_map/ppermute | solution.py:465
  39.9 0.0 collective-permute-done.6.refs_7_
  39.9 6.9 %shard_map.105 = (bf16[4,128,640]{2,1,0:T(8,128)(2,1)S(1)}, bf16[4,128,640]{2,1,0:T(8,128)(2,1)S(1)}, bf16[128,640]{1,0:T(8,128)(2,1)S(1)}, bf16[128,640]{1,0:T(...) custom-call(bf16[4,128,640]{2,1,0:T(8,128)(2,1)S(1)} %copy-done.5, ...), custom_call_target="tpu_custom_call" | custom-call | bytes 1 | tf_op jit(solution)/shard_map/pallas_call | solution.py:297
  46.9 2.0 %collective-permute-start.11 = (bf16[128,640]{1,0:T(8,128)(2,1)S(1)}, bf16[128,640]{1,0:T(8,128)(2,1)S(1)}, u32[]{:S(2)}, u32[]{:S(2)}) collective-permute-start(bf16[128,640]{1,0:T(8,128)(2,1)S(1)} %get-tuple-element.85), channel_id=1, source_target_pairs={{0,4},{2,6},{4,0},{6,2},{1,5},{3,7},{5,1},{7,3},{8,12},{10,14},{12... | collective-permute-start | bytes 491528 | tf_op jit(solution)/shard_map/ppermute | solution.py:465
  48.8 2.3 %collective-permute-start.12 = (bf16[128,640]{1,0:T(8,128)(2,1)S(1)}, bf16[128,640]{1,0:T(8,128)(2,1)S(1)}, u32[]{:S(2)}, u32[]{:S(2)}) collective-permute-start(bf16[128,640]{1,0:T(8,128)(2,1)S(1)} %get-tuple-element.86), channel_id=1, source_target_pairs={{0,6},{2,4},{4,2},{6,0},{1,7},{3,5},{5,3},{7,1},{8,14},{10,12},{12... | collective-permute-start | bytes 491528 | tf_op jit(solution)/shard_map/ppermute | solution.py:465
  51.1 0.0 collective-permute-done.4.refs_2_
  51.1 0.0 collective-permute-done.5.refs_3_
  51.2 4.4 %shard_map.106 = (bf16[4,128,384]{2,1,0:T(8,128)(2,1)S(1)}, bf16[4,128,384]{2,1,0:T(8,128)(2,1)S(1)}, bf16[128,384]{1,0:T(8,128)(2,1)S(1)}, bf16[128,384]{1,0:T(...) custom-call(bf16[4,128,384]{2,1,0:T(8,128)(2,1)S(1)} %copy-done.7, ...), custom_call_target="tpu_custom_call", output_to_operand_aliasing={{4}: (10, {})} | custom-call | flops 34359738368 | bytes 1 | tf_op jit(solution)/shard_map/pallas_call | solution.py:297
  55.5 0.0 copy-start
  55.6 0.0 copy-start.1
  55.6 0.0 copy-start.2
  55.6 6.4 %collective-permute-done.11.refs_2_ = bf16[128,640]{1,0:T(8,128)(2,1)S(1)} collective-permute-done((bf16[128,640]{1,0:T(8,128)(2,1)S(1)}, bf16[128,640]{1,0:T(8,128)(2,1)S(1)}, u32[]{:S(2)}, u32[]{:S(2)}) %collective-permute-start.11) | collective-permute-done | bytes 163872 | tf_op jit(solution)/shard_map/ppermute | solution.py:465
  61.9 0.0 collective-permute-start.15
  61.9 0.5 collective-permute-start.17
  62.5 0.0 collective-permute-start.13
  62.5 0.5 collective-permute-start.14
  63.0 0.3 collective-permute-done.15.refs_2_
  63.2 0.2 collective-permute-start.16
  63.4 3.4 %collective-permute-start.7 = (bf16[4,128,384]{2,1,0:T(8,128)(2,1)S(1)}, bf16[4,128,384]{2,1,0:T(8,128)(2,1)S(1)}, u32[]{:S(2)}, u32[]{:S(2)}) collective-permute-start(bf16[4,128,384]{2,1,0:T(8,128)(2,1)S(1)} %get-tuple-element.75), channel_id=1, source_target_pairs={{0,2},{2,0},{4,6},{6,4},{1,3},{3,1},{5,7},{7,5},{8,10},{10,8},{12,... | collective-permute-start | bytes 1179656 | tf_op jit(solution)/shard_map/ppermute | solution.py:462
  66.8 0.0 collective-permute-done.13.refs_0_
  66.8 0.0 collective-permute-done.14.refs_1_
  66.8 0.0 collective-permute-done.16.refs_3_
  66.8 0.2 shard_map.109
  67.0 1.6 %collective-permute-start.18 = (bf16[64,1024]{1,0:T(8,128)(2,1)S(1)}, bf16[64,1024]{1,0:T(8,128)(2,1)S(1)}, u32[]{:S(2)}, u32[]{:S(2)}) collective-permute-start(bf16[64,1024]{1,0:T(8,128)(2,1)S(1)} %get-tuple-element.103), channel_id=1, source_target_pairs={{0,16},{8,24},{16,0},{24,8},{1,17},{9,25},{17,1},{25,9},{2,18},{10... | collective-permute-start | bytes 393224 | tf_op jit(solution)/shard_map/ppermute | solution.py:440
  68.6 3.9 %collective-permute-done.18.arrived = bf16[64,1024]{1,0:T(8,128)(2,1)S(1)} collective-permute-done((bf16[64,1024]{1,0:T(8,128)(2,1)S(1)}, bf16[64,1024]{1,0:T(8,128)(2,1)S(1)}, u32[]{:S(2)}, u32[]{:S(2)}) %collective-permute-start.18) | collective-permute-done | bytes 131104 | tf_op jit(solution)/shard_map/ppermute | solution.py:440
  72.6 2.1 %collective-permute-start.19 = (bf16[64,1024]{1,0:T(8,128)(2,1)S(1)}, bf16[64,1024]{1,0:T(8,128)(2,1)S(1)}, u32[]{:S(2)}, u32[]{:S(2)}) collective-permute-start(bf16[64,1024]{1,0:T(8,128)(2,1)S(1)} %shard_map.110), channel_id=1, source_target_pairs={{0,4},{2,6},{4,0},{6,2},{1,5},{3,7},{5,1},{7,3},{8,12},{10,14},{12... | collective-permute-start | bytes 393224 | tf_op jit(solution)/shard_map/ppermute | solution.py:442
  74.7 0.9 collective-permute-start.8
  75.6 2.2 %collective-permute-start.9 = (bf16[128,384]{1,0:T(8,128)(2,1)S(1)}, bf16[128,384]{1,0:T(8,128)(2,1)S(1)}, u32[]{:S(2)}, u32[]{:S(2)}) collective-permute-start(bf16[128,384]{1,0:T(8,128)(2,1)S(1)} %get-tuple-element.77), channel_id=1, source_target_pairs={{0,6},{2,4},{4,2},{6,0},{1,7},{3,5},{5,3},{7,1},{8,14},{10,12},{12... | collective-permute-start | bytes 294920 | tf_op jit(solution)/shard_map/ppermute | solution.py:465
  77.7 4.5 %collective-permute-done.19.over = bf16[64,1024]{1,0:T(8,128)(2,1)S(1)} collective-permute-done((bf16[64,1024]{1,0:T(8,128)(2,1)S(1)}, bf16[64,1024]{1,0:T(8,128)(2,1)S(1)}, u32[]{:S(2)}, u32[]{:S(2)}) %collective-permute-start.19) | collective-permute-done | bytes 131104 | tf_op jit(solution)/shard_map/ppermute | solution.py:442
  82.3 0.1 shard_map.111
  82.4 1.6 %collective-permute-start.20 = (bf16[128,1024]{1,0:T(8,128)(2,1)S(1)}, bf16[128,1024]{1,0:T(8,128)(2,1)S(1)}, u32[]{:S(2)}, u32[]{:S(2)}) collective-permute-start(bf16[128,1024]{1,0:T(8,128)(2,1)S(1)} %get-tuple-element.105), channel_id=1, source_target_pairs={{0,16},{8,24},{16,0},{24,8},{1,17},{9,25},{17,1},{25,9},{2,18},{10... | collective-permute-start | bytes 786440 | tf_op jit(solution)/shard_map/ppermute | solution.py:448
  84.0 1.5 %shard_map.107 = (bf16[128,4096]{1,0:T(8,128)(2,1)}, bf16[128,4096]{1,0:T(8,128)(2,1)}, bf16[128,4096]{1,0:T(8,128)(2,1)}) custom-call(bf16[4,128,640]{2,1,0:T(8,128)(2,1)S(1)} %get-tuple-element.78.refs_0_, bf16[4,128,640]{2,1,0:T(8,128)(2,1)S(1)} %collective-permute-done.10.refs_1_, bf16[128,640]{1,0:T(8,128)(2,1)S(1)} %collective-permute-done.11.refs_2_, ...), custom_call_target="tpu_custom_call" | custom-call | bytes 1 | tf_op jit(solution)/shard_map/pallas_call | solution.py:341
  85.5 3.2 %collective-permute-done.8.refs_2_ = bf16[128,384]{1,0:T(8,128)(2,1)S(1)} collective-permute-done((bf16[128,384]{1,0:T(8,128)(2,1)S(1)}, bf16[128,384]{1,0:T(8,128)(2,1)S(1)}, u32[]{:S(2)}, u32[]{:S(2)}) %collective-permute-start.8) | collective-permute-done | bytes 98336 | tf_op jit(solution)/shard_map/ppermute | solution.py:465
  88.7 1.2 %shard_map.108 = (bf16[128,4096]{1,0:T(8,128)(2,1)}, bf16[128,4096]{1,0:T(8,128)(2,1)}, bf16[128,4096]{1,0:T(8,128)(2,1)}) custom-call(bf16[4,128,384]{2,1,0:T(8,128)(2,1)S(1)} %get-tuple-element.74.refs_0_, bf16[4,128,384]{2,1,0:T(8,128)(2,1)S(1)} %collective-permute-done.7.refs_1_, ...), custom_call_target="tpu_custom_call", output_to_operand_aliasing={{0}: (7, {}), {1}: (8, {}), {2}: (9, {})} | custom-call | flops 34359738368 | bytes 1 | tf_op jit(solution)/shard_map/pallas_call | solution.py:341
  89.9 0.8 shard_map.112
  (26 shorter events, 0.1 us)
Async XLA Ops:
  4.0 34.0 %collective-permute-start.1 = (bf16[4,128,640]{2,1,0:T(8,128)(2,1)}, bf16[4,128,640]{2,1,0:T(8,128)(2,1)S(1)}, u32[]{:S(2)}, u32[]{:S(2)}) collective-permute-start(bf16[4,128,640]{2,1,0:T(8,128)(2,1)} %get-tuple-element.60), channel_id=1, source_target_pairs={{0,2},{2,0},{4,6},{6,4},{1,3},{3,1},{5,7},{7,5},{8,10},{10,8},{12,... | collective-permute-start | bytes 1966088 | tf_op jit(solution)/shard_map/ppermute | solution.py:462
  7.1 30.9 %collective-permute-start.2 = (bf16[1664,128]{1,0:T(8,128)(2,1)}, bf16[1664,128]{1,0:T(8,128)(2,1)S(1)}, u32[]{:S(2)}, u32[]{:S(2)}) collective-permute-start(bf16[1664,128]{1,0:T(8,128)(2,1)} %get-tuple-element.61), channel_id=1, source_target_pairs={{0,4},{2,6},{4,0},{6,2},{1,5},{3,7},{5,1},{7,3},{8,12},{10,14},{12... | collective-permute-start | bytes 1277960 | tf_op jit(solution)/shard_map/ppermute | solution.py:465
  9.7 3.8 %copy-start.3 = (f32[512,1024]{1,0:T(8,128)S(1)}, f32[512,1024]{1,0:T(8,128)}, u32[]{:S(2)}) copy-start(f32[512,1024]{1,0:T(8,128)} %taps.1) | copy-start | bytes 6291460
  9.7 3.8 %copy-start.4 = (bf16[2048,256]{1,0:T(8,128)(2,1)S(1)}, bf16[2048,256]{1,0:T(8,128)(2,1)}, u32[]{:S(2)}) copy-start(bf16[2048,256]{1,0:T(8,128)(2,1)} %constant.4.clone.fwd.refs_8_) | copy-start | bytes 3145732
  9.7 28.3 %collective-permute-start.3 = (bf16[128,640]{1,0:T(8,128)(2,1)}, bf16[128,640]{1,0:T(8,128)(2,1)S(1)}, u32[]{:S(2)}, u32[]{:S(2)}) collective-permute-start(bf16[128,640]{1,0:T(8,128)(2,1)} %get-tuple-element.62), channel_id=1, source_target_pairs={{0,6},{2,4},{4,2},{6,0},{1,7},{3,5},{5,3},{7,1},{8,14},{10,12},{12... | collective-permute-start | bytes 491528 | tf_op jit(solution)/shard_map/ppermute | solution.py:465
  12.4 25.7 %copy-start.9 = (bf16[128,384]{1,0:T(8,128)(2,1)S(1)}, bf16[128,384]{1,0:T(8,128)(2,1)}, u32[]{:S(2)}) copy-start(bf16[128,384]{1,0:T(8,128)(2,1)} %get-tuple-element.65) | copy-start | bytes 294916
  12.4 25.8 %copy-start.8 = (bf16[128,384]{1,0:T(8,128)(2,1)S(1)}, bf16[128,384]{1,0:T(8,128)(2,1)}, u32[]{:S(2)}) copy-start(bf16[128,384]{1,0:T(8,128)(2,1)} %get-tuple-element.66) | copy-start | bytes 294916
  12.4 27.4 %copy-start.5 = (bf16[4,128,640]{2,1,0:T(8,128)(2,1)S(1)}, bf16[4,128,640]{2,1,0:T(8,128)(2,1)}, u32[]{:S(2)}) copy-start(bf16[4,128,640]{2,1,0:T(8,128)(2,1)} %get-tuple-element.70.refs_0_) | copy-start | bytes 1966084
  12.5 27.4 %copy-start.6 = (bf16[512,512]{1,0:T(8,128)(2,1)S(1)}, bf16[512,512]{1,0:T(8,128)(2,1)}, u32[]{:S(2)}) copy-start(bf16[512,512]{1,0:T(8,128)(2,1)} %constant.5.clone.refs_9_) | copy-start | bytes 1572868
  12.5 38.7 %collective-permute-start = (bf16[4,128,384]{2,1,0:T(8,128)(2,1)}, bf16[4,128,384]{2,1,0:T(8,128)(2,1)S(1)}, u32[]{:S(2)}, u32[]{:S(2)}) collective-permute-start(bf16[4,128,384]{2,1,0:T(8,128)(2,1)} %get-tuple-element.56), channel_id=1, source_target_pairs={{0,2},{2,0},{4,6},{6,4},{1,3},{3,1},{5,7},{7,5},{8,10},{10,8},{12,... | collective-permute-start | bytes 1179656 | tf_op jit(solution)/shard_map/ppermute | solution.py:462
  38.1 13.1 %copy-start.7 = (bf16[4,128,384]{2,1,0:T(8,128)(2,1)S(1)}, bf16[4,128,384]{2,1,0:T(8,128)(2,1)}, u32[]{:S(2)}) copy-start(bf16[4,128,384]{2,1,0:T(8,128)(2,1)} %get-tuple-element.55.refs_0_) | copy-start | bytes 1179652
  38.1 1.8 %collective-permute-start.6 = (bf16[1024,128]{1,0:T(8,128)(2,1)S(1)}, bf16[1024,128]{1,0:T(8,128)(2,1)S(1)}, u32[]{:S(2)}, u32[]{:S(2)}) collective-permute-start(bf16[1024,128]{1,0:T(8,128)(2,1)S(1)} %slice.3), channel_id=1, source_target_pairs={{0,8},{8,0},{16,24},{24,16},{1,9},{9,1},{17,25},{25,17},{2,10},{10... | collective-permute-start | bytes 786440 | tf_op jit(solution)/shard_map/ppermute | solution.py:486
  38.2 13.0 %collective-permute-start.4 = (bf16[128,384]{1,0:T(8,128)(2,1)S(1)}, bf16[128,384]{1,0:T(8,128)(2,1)S(1)}, u32[]{:S(2)}, u32[]{:S(2)}) collective-permute-start(bf16[128,384]{1,0:T(8,128)(2,1)S(1)} %copy-done.9), channel_id=1, source_target_pairs={{0,4},{2,6},{4,0},{6,2},{1,5},{3,7},{5,1},{7,3},{8,12},{10,14},{12... | collective-permute-start | bytes 294920 | tf_op jit(solution)/shard_map/ppermute | solution.py:465
  38.3 12.9 %collective-permute-start.5 = (bf16[128,384]{1,0:T(8,128)(2,1)S(1)}, bf16[128,384]{1,0:T(8,128)(2,1)S(1)}, u32[]{:S(2)}, u32[]{:S(2)}) collective-permute-start(bf16[128,384]{1,0:T(8,128)(2,1)S(1)} %copy-done.8), channel_id=1, source_target_pairs={{0,6},{2,4},{4,2},{6,0},{1,7},{3,5},{5,3},{7,1},{8,14},{10,12},{12... | collective-permute-start | bytes 294920 | tf_op jit(solution)/shard_map/ppermute | solution.py:465
  46.9 15.1 %collective-permute-start.11 = (bf16[128,640]{1,0:T(8,128)(2,1)S(1)}, bf16[128,640]{1,0:T(8,128)(2,1)S(1)}, u32[]{:S(2)}, u32[]{:S(2)}) collective-permute-start(bf16[128,640]{1,0:T(8,128)(2,1)S(1)} %get-tuple-element.85), channel_id=1, source_target_pairs={{0,4},{2,6},{4,0},{6,2},{1,5},{3,7},{5,1},{7,3},{8,12},{10,14},{12... | collective-permute-start | bytes 491528 | tf_op jit(solution)/shard_map/ppermute | solution.py:465
  48.8 13.1 %collective-permute-start.12 = (bf16[128,640]{1,0:T(8,128)(2,1)S(1)}, bf16[128,640]{1,0:T(8,128)(2,1)S(1)}, u32[]{:S(2)}, u32[]{:S(2)}) collective-permute-start(bf16[128,640]{1,0:T(8,128)(2,1)S(1)} %get-tuple-element.86), channel_id=1, source_target_pairs={{0,6},{2,4},{4,2},{6,0},{1,7},{3,5},{5,3},{7,1},{8,14},{10,12},{12... | collective-permute-start | bytes 491528 | tf_op jit(solution)/shard_map/ppermute | solution.py:465
  51.1 32.9 %collective-permute-start.10 = (bf16[4,128,640]{2,1,0:T(8,128)(2,1)S(1)}, bf16[4,128,640]{2,1,0:T(8,128)(2,1)S(1)}, u32[]{:S(2)}, u32[]{:S(2)}) collective-permute-start(bf16[4,128,640]{2,1,0:T(8,128)(2,1)S(1)} %get-tuple-element.79), channel_id=1, source_target_pairs={{0,2},{2,0},{4,6},{6,4},{1,3},{3,1},{5,7},{7,5},{8,10},{10,8},{12,... | collective-permute-start | bytes 1966088 | tf_op jit(solution)/shard_map/ppermute | solution.py:462
  55.5 28.4 %copy-start = (bf16[128,4096]{1,0:T(8,128)(2,1)S(1)}, bf16[128,4096]{1,0:T(8,128)(2,1)}, u32[]{:S(2)}) copy-start(bf16[128,4096]{1,0:T(8,128)(2,1)} %refs_6_.3) | copy-start | bytes 3145732
  55.6 28.4 %copy-start.1 = (bf16[128,4096]{1,0:T(8,128)(2,1)S(1)}, bf16[128,4096]{1,0:T(8,128)(2,1)}, u32[]{:S(2)}) copy-start(bf16[128,4096]{1,0:T(8,128)(2,1)} %refs_5_.3) | copy-start | bytes 3145732
  55.6 28.4 %copy-start.2 = (bf16[128,4096]{1,0:T(8,128)(2,1)S(1)}, bf16[128,4096]{1,0:T(8,128)(2,1)}, u32[]{:S(2)}) copy-start(bf16[128,4096]{1,0:T(8,128)(2,1)} %refs_4_.5) | copy-start | bytes 3145732
  61.9 1.3 %collective-permute-start.15 = (bf16[384,128]{1,0:T(8,128)(2,1)S(1)}, bf16[384,128]{1,0:T(8,128)(2,1)S(1)}, u32[]{:S(2)}, u32[]{:S(2)}) collective-permute-start(bf16[384,128]{1,0:T(8,128)(2,1)S(1)} %get-tuple-element.98), channel_id=1, source_target_pairs={{0,8},{8,0},{16,24},{24,16},{1,9},{9,1},{17,25},{25,17},{2,10},{10... | collective-permute-start | bytes 294920 | tf_op jit(solution)/shard_map/ppermute | solution.py:418
  61.9 1.5 %collective-permute-start.17 = (bf16[384,128]{1,0:T(8,128)(2,1)S(1)}, bf16[384,128]{1,0:T(8,128)(2,1)S(1)}, u32[]{:S(2)}, u32[]{:S(2)}) collective-permute-start(bf16[384,128]{1,0:T(8,128)(2,1)S(1)} %get-tuple-element.100), channel_id=1, source_target_pairs={{0,8},{8,0},{16,24},{24,16},{1,9},{9,1},{17,25},{25,17},{2,10},{10... | collective-permute-start | bytes 294920 | tf_op jit(solution)/shard_map/ppermute | solution.py:418
  62.5 4.3 %collective-permute-start.13 = (bf16[384,256]{1,0:T(8,128)(2,1)S(1)}, bf16[384,256]{1,0:T(8,128)(2,1)S(1)}, u32[]{:S(2)}, u32[]{:S(2)}) collective-permute-start(bf16[384,256]{1,0:T(8,128)(2,1)S(1)} %get-tuple-element.96), channel_id=1, source_target_pairs={{0,8},{8,0},{16,24},{24,16},{1,9},{9,1},{17,25},{25,17},{2,10},{10... | collective-permute-start | bytes 589832 | tf_op jit(solution)/shard_map/ppermute | solution.py:418
  62.5 4.3 %collective-permute-start.14 = (bf16[384,256]{1,0:T(8,128)(2,1)S(1)}, bf16[384,256]{1,0:T(8,128)(2,1)S(1)}, u32[]{:S(2)}, u32[]{:S(2)}) collective-permute-start(bf16[384,256]{1,0:T(8,128)(2,1)S(1)} %get-tuple-element.97), channel_id=1, source_target_pairs={{0,8},{8,0},{16,24},{24,16},{1,9},{9,1},{17,25},{25,17},{2,10},{10... | collective-permute-start | bytes 589832 | tf_op jit(solution)/shard_map/ppermute | solution.py:418
  63.2 3.5 %collective-permute-start.16 = (bf16[384,256]{1,0:T(8,128)(2,1)S(1)}, bf16[384,256]{1,0:T(8,128)(2,1)S(1)}, u32[]{:S(2)}, u32[]{:S(2)}) collective-permute-start(bf16[384,256]{1,0:T(8,128)(2,1)S(1)} %get-tuple-element.99), channel_id=1, source_target_pairs={{0,8},{8,0},{16,24},{24,16},{1,9},{9,1},{17,25},{25,17},{2,10},{10... | collective-permute-start | bytes 589832 | tf_op jit(solution)/shard_map/ppermute | solution.py:418
  63.4 25.3 %collective-permute-start.7 = (bf16[4,128,384]{2,1,0:T(8,128)(2,1)S(1)}, bf16[4,128,384]{2,1,0:T(8,128)(2,1)S(1)}, u32[]{:S(2)}, u32[]{:S(2)}) collective-permute-start(bf16[4,128,384]{2,1,0:T(8,128)(2,1)S(1)} %get-tuple-element.75), channel_id=1, source_target_pairs={{0,2},{2,0},{4,6},{6,4},{1,3},{3,1},{5,7},{7,5},{8,10},{10,8},{12,... | collective-permute-start | bytes 1179656 | tf_op jit(solution)/shard_map/ppermute | solution.py:462
  67.0 5.5 %collective-permute-start.18 = (bf16[64,1024]{1,0:T(8,128)(2,1)S(1)}, bf16[64,1024]{1,0:T(8,128)(2,1)S(1)}, u32[]{:S(2)}, u32[]{:S(2)}) collective-permute-start(bf16[64,1024]{1,0:T(8,128)(2,1)S(1)} %get-tuple-element.103), channel_id=1, source_target_pairs={{0,16},{8,24},{16,0},{24,8},{1,17},{9,25},{17,1},{25,9},{2,18},{10... | collective-permute-start | bytes 393224 | tf_op jit(solution)/shard_map/ppermute | solution.py:440
  72.6 9.7 %collective-permute-start.19 = (bf16[64,1024]{1,0:T(8,128)(2,1)S(1)}, bf16[64,1024]{1,0:T(8,128)(2,1)S(1)}, u32[]{:S(2)}, u32[]{:S(2)}) collective-permute-start(bf16[64,1024]{1,0:T(8,128)(2,1)S(1)} %shard_map.110), channel_id=1, source_target_pairs={{0,4},{2,6},{4,0},{6,2},{1,5},{3,7},{5,1},{7,3},{8,12},{10,14},{12... | collective-permute-start | bytes 393224 | tf_op jit(solution)/shard_map/ppermute | solution.py:442
  74.7 14.0 %collective-permute-start.8 = (bf16[128,384]{1,0:T(8,128)(2,1)S(1)}, bf16[128,384]{1,0:T(8,128)(2,1)S(1)}, u32[]{:S(2)}, u32[]{:S(2)}) collective-permute-start(bf16[128,384]{1,0:T(8,128)(2,1)S(1)} %get-tuple-element.76), channel_id=1, source_target_pairs={{0,4},{2,6},{4,0},{6,2},{1,5},{3,7},{5,1},{7,3},{8,12},{10,14},{12... | collective-permute-start | bytes 294920 | tf_op jit(solution)/shard_map/ppermute | solution.py:465
  75.6 13.1 %collective-permute-start.9 = (bf16[128,384]{1,0:T(8,128)(2,1)S(1)}, bf16[128,384]{1,0:T(8,128)(2,1)S(1)}, u32[]{:S(2)}, u32[]{:S(2)}) collective-permute-start(bf16[128,384]{1,0:T(8,128)(2,1)S(1)} %get-tuple-element.77), channel_id=1, source_target_pairs={{0,6},{2,4},{4,2},{6,0},{1,7},{3,5},{5,3},{7,1},{8,14},{10,12},{12... | collective-permute-start | bytes 294920 | tf_op jit(solution)/shard_map/ppermute | solution.py:465
  82.4 7.5 %collective-permute-start.20 = (bf16[128,1024]{1,0:T(8,128)(2,1)S(1)}, bf16[128,1024]{1,0:T(8,128)(2,1)S(1)}, u32[]{:S(2)}, u32[]{:S(2)}) collective-permute-start(bf16[128,1024]{1,0:T(8,128)(2,1)S(1)} %get-tuple-element.105), channel_id=1, source_target_pairs={{0,16},{8,24},{16,0},{24,8},{1,17},{9,25},{17,1},{25,9},{2,18},{10... | collective-permute-start | bytes 786440 | tf_op jit(solution)/shard_map/ppermute | solution.py:448
